TPU v7x, 512 devices: a whole 4x4x16 slice. The times are simulated.
512 devices in a mesh: slot: 64 (over y, z), hid: 8 (over x, core).
Axes of the slice: x: 4, y: 4, z: 16, core: 2. Of those that a mesh axis runs over, the one named last changes fastest.
Arguments:
- inputs: bfloat16 [64, 512, 4096], P('slot', None, 'hid'), may hold values from -6 to 6
- cotangent: bfloat16 [64, 512, 4096], P('slot', None, 'hid'), may hold values from -6 to 6
- w_gate: bfloat16 [64, 768, 4096], P('slot', 'hid'), may hold values from -0.09375 to 0.09375
- w_up: bfloat16 [64, 768, 4096], P('slot', 'hid'), may hold values from -0.09375 to 0.09375
- counts: int32 [64], replicated, may hold values from 1 to 512, 24576 in all
- place_now: int32 [64, 1], replicated, may hold values from 0 to 11
- place_next: int32 [64, 1], replicated, may hold values from 0 to 11
- master: float32 [12, 768, 4096], P(None, 'slot', 'hid'), may hold values from -0.21875 to 0.21875
- moment_one: float32 [12, 768, 4096], P(None, 'slot', 'hid'), may hold values from -0.3125 to 0.3125
- moment_two: float32 [12, 768, 4096], P(None, 'slot', 'hid'), may hold values from 0.0001 to 0.01
Outputs:
- new_master: float32 [12, 768, 4096], P(None, 'slot', 'hid')
- new_one: float32 [12, 768, 4096], P(None, 'slot', 'hid')
- new_two: float32 [12, 768, 4096], P(None, 'slot', 'hid')
- next_down: bfloat16 [64, 768, 4096], P('slot', 'hid')
Inputs may be any that keep to these rules, and one draw needn't show every extreme that they name: `counts`: rows of a slot at or past its count are padding; some slot is full. `place_now`: every expert is held by at least one slot. `place_next`: every expert is held by at least one slot.
All inputs are finite; a program needn't handle non-finite values.
Results may differ from a plain program's by a relative error of at most 0.002.
Values may be sent and summed in bfloat16 or wider, within the bound.
A program may use at most 64 MiB of HBM per device.

v0:
```python
from functools import reduce

import jax
import jax.numpy as jnp
from jax import lax
from jax.sharding import PartitionSpec as P

STEP = 100


def by_blocks(make, total):
    results = []
    for begin in range(0, total, 128):
        results.append(make(begin))
    return results


def contract_rows(left, right):
    return lax.dot_general(
        left, right, (((0,), (0,)), ((), ())), preferred_element_type=jnp.float32
    )


def contract_cols(left, right):
    return lax.dot_general(
        left, right, (((1,), (1,)), ((), ())), preferred_element_type=jnp.float32
    )


def local(
    inputs, cotangent, w_gate, w_up, counts, place_now, place_next, master, moment_one, moment_two
):
    capacity = inputs.shape[1]
    ff_local = w_gate.shape[1]
    slot_id = lax.axis_index("slot")
    count = lax.dynamic_index_in_dim(counts, slot_id, 0, keepdims=False)
    piece = lax.all_gather(inputs, "hid", axis=2, tiled=True)
    gate_cols = w_gate[0]
    up_cols = w_up[0]

    def make(lo):
        block = lax.dynamic_slice_in_dim(piece[0], lo, 128, 0)
        return jnp.concatenate(
            [contract_cols(block, gate_cols), contract_cols(block, up_cols)], axis=1
        )

    both = jnp.concatenate(by_blocks(make, capacity), axis=0)
    gate = both[:, :ff_local]
    up = both[:, ff_local:]
    hidden = (jax.nn.silu(gate) * up).astype(jnp.bfloat16)
    row_ids = jnp.arange(capacity, dtype=jnp.int32)
    masked_hidden = jnp.where((row_ids < count)[:, None], hidden, jnp.zeros_like(hidden))
    column_piece = lax.all_gather(cotangent, "hid", axis=2, tiled=True)

    def make(lo):
        left = lax.dynamic_slice_in_dim(masked_hidden, lo, 128, 0)
        right = lax.dynamic_slice_in_dim(column_piece[0], lo, 128, 0)
        return contract_rows(left, right)

    slot_grad = reduce(jnp.add, by_blocks(make, capacity))
    column_grad = lax.all_to_all(
        slot_grad.astype(jnp.bfloat16), "hid", split_axis=1, concat_axis=0, tiled=True
    ).astype(slot_grad.dtype)
    received = lax.all_to_all(
        column_grad.astype(jnp.bfloat16), "slot", split_axis=0, concat_axis=0, tiled=True
    ).astype(column_grad.dtype)
    slots = counts.shape[0]
    experts = master.shape[0]
    ff_shard = master.shape[1]
    columns = master.shape[2]
    received = received.reshape(slots, ff_shard, columns)
    experts_now = place_now[:, 0]
    match = experts_now[None, :] == jnp.arange(experts, dtype=jnp.int32)[:, None]
    selector = match.astype(jnp.float32)
    summed = jnp.einsum("es,sfc->efc", selector, received, precision=lax.Precision.HIGHEST)
    rows = jnp.sum(jnp.where(match, counts[None, :], 0), axis=1)
    grad = summed / rows.astype(jnp.float32)[:, None, None]
    new_one = 0.9 * moment_one + 0.1 * grad
    new_two = 0.95 * moment_two + 0.05 * grad * grad
    fixed_one = 1.0 - 0.9**STEP
    fixed_two = 1.0 - 0.95**STEP
    new_master = master - 0.01 * (new_one / fixed_one) / (jnp.sqrt(new_two / fixed_two) + 1e-08)
    outgoing = jnp.take(new_master.astype(jnp.bfloat16), place_next[:, 0], axis=0)
    next_down = lax.all_to_all(
        lax.all_to_all(outgoing, "slot", split_axis=0, concat_axis=1, tiled=True),
        "hid",
        split_axis=1,
        concat_axis=2,
        tiled=True,
    )
    return (new_master, new_one, new_two, next_down)


def solution(mesh):
    return jax.shard_map(
        local,
        mesh=mesh,
        in_specs=(
            P("slot", None, "hid"),
            P("slot", None, "hid"),
            P("slot", "hid", None),
            P("slot", "hid", None),
            P(),
            P(),
            P(),
            P(None, "slot", "hid"),
            P(None, "slot", "hid"),
            P(None, "slot", "hid"),
        ),
        out_specs=(
            P(None, "slot", "hid"),
            P(None, "slot", "hid"),
            P(None, "slot", "hid"),
            P("slot", "hid", None),
        ),
        check_vma=False,
    )
```

profile of v0, /device:TPU:1, one launch (start us, length us, event | category | flops | bytes accessed | tf_op | source)
XLA Modules:
  0.0 284.6 jit_solution(15138740714693062401)
XLA Ops:
  7.2 0.7 all-gather.3.cloned.1.call-update
  8.0 0.7 all-gather.5.cloned.1.call-update
  8.7 1.2 dynamic_slice.56
  9.9 0.6 iota_compare_fusion.1
  10.6 45.1 %all-gather.3.cloned.1.call-done = bf16[1,512,4096]{2,1,0:T(8,128)(2,1)} async-done(((bf16[1,512,512]{2,1,0:T(8,128)(2,1)}), bf16[1,512,4096]{2,1,0:T(8,128)(2,1)}) %all-gather.3.cloned.1.call-update) | async-done | bytes 4194320 | tf_op jit(solution)/shard_map/all_gather | solution.py:37
  55.7 1.8 fusion.2
  57.5 1.7 fusion.4
  59.2 1.7 fusion.3
  61.0 0.5 fusion.5
  61.9 0.5 fusion.7
  62.9 0.5 fusion.9
  63.5 34.1 %all-gather.5.cloned.1.call-done = bf16[1,512,4096]{2,1,0:T(8,128)(2,1)} async-done(((bf16[1,512,512]{2,1,0:T(8,128)(2,1)}), bf16[1,512,4096]{2,1,0:T(8,128)(2,1)}) %all-gather.5.cloned.1.call-update) | async-done | bytes 4194320 | tf_op jit(solution)/shard_map/all_gather | solution.py:53
  97.6 1.7 fusion.1
  99.4 1.6 convolution_add_fusion.2
  101.9 15.4 %all_to_all.56 = bf16[96,8,512]{2,0,1:T(8,128)(2,1)S(1)} all-to-all(bf16[96,8,512]{2,0,1:T(8,128)(2,1)S(1)} %bitcast.72), channel_id=1, replica_groups=mesh['slot'=64,'hid'=8] {'hid'}, dimensions={1} | all-to-all | bytes 1572864 | tf_op jit(solution)/shard_map/all_to_all | solution.py:61
  117.2 1.2 all_to_all.43
  118.4 15.4 %all-to-all-start.1 = ((bf16[64,12,512]{2,1,0:T(8,128)(2,1)}), bf16[64,12,512]{2,1,0:T(8,128)(2,1)S(1)}, u32[]{:S(2)}, u32[]{:S(2)}) async-start(bf16[64,12,512]{2,1,0:T(8,128)(2,1)} %all_to_all.43), calls=%async_computation.1 | async-start | bytes 2097152 | tf_op jit(solution)/shard_map/all_to_all | solution.py:64
  133.9 49.9 %all-to-all-done.1 = bf16[64,12,512]{2,1,0:T(8,128)(2,1)S(1)} async-done(((bf16[64,12,512]{2,1,0:T(8,128)(2,1)}), bf16[64,12,512]{2,1,0:T(8,128)(2,1)S(1)}, u32[]{:S(2)}, u32[]{:S(2)}) %all-to-all-start.1) | async-done | bytes 786464 | tf_op jit(solution)/shard_map/all_to_all | solution.py:64
  183.8 2.5 fusion.30
  186.4 0.6 gather_fusion
  187.2 60.6 %all_to_all.57 = bf16[64,12,512]{2,1,0:T(8,128)(2,1)S(1)} all-to-all(bf16[64,12,512]{2,1,0:T(8,128)(2,1)S(1)} %broadcast_select_fusion), channel_id=1, replica_groups=mesh['slot'=64,'hid'=8] {'slot'}, dimensions={0} | all-to-all | bytes 1572864 | tf_op jit(solution)/shard_map/all_to_all | solution.py:85
  247.8 0.5 all_to_all.51
  248.3 0.5 broadcast.23
  248.8 5.4 %reduce = bf16[768,512]{1,0:T(8,128)(2,1)S(1)} reduce(bf16[768,1,512]{2,1,0:T(2,128)(2,1)S(1)} %bitcast.69, bf16[]{:T(256)} %broadcast.23), dimensions={1}, to_apply=%bitcast.64.reduce_sub_computation | reduce | bytes 1572866
  254.3 1.5 reshape.49
  255.8 7.7 %all-to-all-start.3 = ((bf16[8,2,24576]{2,1,0:T(2,128)(2,1)}), bf16[8,2,24576]{2,1,0:T(2,128)(2,1)S(1)}, u32[]{:S(2)}, u32[]{:S(2)}) async-start(bf16[8,2,24576]{2,1,0:T(2,128)(2,1)} %reshape.49), calls=%async_computation.3 | async-start | bytes 1572864 | tf_op jit(solution)/shard_map/all_to_all | solution.py:84
  263.4 1.9 copy.47
  265.3 0.9 copy.48
  266.3 0.9 copy.49
  267.2 8.5 %all-to-all-done.3 = bf16[8,2,24576]{2,1,0:T(2,128)(2,1)S(1)} async-done(((bf16[8,2,24576]{2,1,0:T(2,128)(2,1)}), bf16[8,2,24576]{2,1,0:T(2,128)(2,1)S(1)}, u32[]{:S(2)}, u32[]{:S(2)}) %all-to-all-start.3) | async-done | bytes 786464 | tf_op jit(solution)/shard_map/all_to_all | solution.py:84
  275.7 0.8 reshape.50
  276.8 1.0 copy.52
  (41 shorter events, 2.6 us)
Async XLA Ops:
  7.2 48.5 %copy-start = (bf16[1,96,4096]{2,1,0:T(8,128)(2,1)S(1)}, bf16[1,96,4096]{2,1,0:T(8,128)(2,1)}, u32[]{:S(2)}) copy-start(bf16[1,96,4096]{2,1,0:T(8,128)(2,1)} %param.13) | copy-start | bytes 2359300
  7.2 52.0 %copy-start.5 = (bf16[1,96,4096]{2,1,0:T(8,128)(2,1)S(1)}, bf16[1,96,4096]{2,1,0:T(8,128)(2,1)}, u32[]{:S(2)}) copy-start(bf16[1,96,4096]{2,1,0:T(8,128)(2,1)} %param.12) | copy-start | bytes 2359300
  7.2 48.5 %all-gather.3.cloned.1.call-start = ((), (), s32[]{:S(2)}) async-start(), calls=%async_computation.4 | async-start | bytes 4718592 | tf_op jit(solution)/shard_map/all_gather | solution.py:37
  7.9 89.7 %all-gather.5.cloned.1.call-start = ((), (), s32[]{:S(2)}) async-start(), calls=%async_computation.5 | async-start | bytes 4718592 | tf_op jit(solution)/shard_map/all_gather | solution.py:53
  55.7 5.3 %copy-start.4 = (bf16[1,512,4096]{2,1,0:T(8,128)(2,1)S(1)}, bf16[1,512,4096]{2,1,0:T(8,128)(2,1)}, u32[]{:S(2)}) copy-start(bf16[1,512,4096]{2,1,0:T(8,128)(2,1)} %all-gather.3.cloned.1.call-done) | copy-start | bytes 12582916
  97.6 3.3 %copy-start.1 = (bf16[1,512,4096]{2,1,0:T(8,128)(2,1)S(1)}, bf16[1,512,4096]{2,1,0:T(8,128)(2,1)}, u32[]{:S(2)}) copy-start(bf16[1,512,4096]{2,1,0:T(8,128)(2,1)} %all-gather.5.cloned.1.call-done) | copy-start | bytes 12582916
  101.7 32.0 %copy-start.9 = (s32[64]{0:T(128)S(1)}, s32[64]{0:T(128)}, u32[]{:S(2)}) copy-start(s32[64]{0:T(128)} %param.14) | copy-start | bytes 772
  101.7 32.0 %copy-start.11 = (s32[64,1]{0,1:T(1,128)S(1)}, s32[64,1]{0,1:T(1,128)}, u32[]{:S(2)}) copy-start(s32[64,1]{0,1:T(1,128)} %param.15) | copy-start | bytes 772
  101.7 32.2 %copy-start.10 = (s32[64,1]{0,1:T(1,128)S(1)}, s32[64,1]{0,1:T(1,128)}, u32[]{:S(2)}) copy-start(s32[64,1]{0,1:T(1,128)} %param.16) | copy-start | bytes 772
  101.8 82.1 %copy-start.6 = (f32[12,12,512]{2,1,0:T(8,128)S(1)}, f32[12,12,512]{2,1,0:T(8,128)}, u32[]{:S(2)}) copy-start(f32[12,12,512]{2,1,0:T(8,128)} %param.17) | copy-start | bytes 884740
  101.8 82.1 %copy-start.7 = (f32[12,12,512]{2,1,0:T(8,128)S(1)}, f32[12,12,512]{2,1,0:T(8,128)}, u32[]{:S(2)}) copy-start(f32[12,12,512]{2,1,0:T(8,128)} %param.18) | copy-start | bytes 884740
  101.8 82.0 %copy-start.8 = (f32[12,12,512]{2,1,0:T(8,128)S(1)}, f32[12,12,512]{2,1,0:T(8,128)}, u32[]{:S(2)}) copy-start(f32[12,12,512]{2,1,0:T(8,128)} %param.19) | copy-start | bytes 884740
  118.4 65.4 %all-to-all-start.1 = ((bf16[64,12,512]{2,1,0:T(8,128)(2,1)}), bf16[64,12,512]{2,1,0:T(8,128)(2,1)S(1)}, u32[]{:S(2)}, u32[]{:S(2)}) async-start(bf16[64,12,512]{2,1,0:T(8,128)(2,1)} %all_to_all.43), calls=%async_computation.1 | async-start | bytes 2097152 | tf_op jit(solution)/shard_map/all_to_all | solution.py:64
  248.3 17.9 %copy-start.2 = (f32[12,12,512]{2,0,1:T(8,128)S(1)}, f32[12,12,512]{2,0,1:T(8,128)}, u32[]{:S(2)}) copy-start(f32[12,12,512]{2,0,1:T(8,128)} %get-tuple-element.23) | copy-start | bytes 884740
  254.3 11.0 %copy-start.3 = (f32[12,12,512]{2,0,1:T(8,128)S(1)}, f32[12,12,512]{2,0,1:T(8,128)}, u32[]{:S(2)}) copy-start(f32[12,12,512]{2,0,1:T(8,128)} %get-tuple-element.22) | copy-start | bytes 884740
  255.8 20.0 %all-to-all-start.3 = ((bf16[8,2,24576]{2,1,0:T(2,128)(2,1)}), bf16[8,2,24576]{2,1,0:T(2,128)(2,1)S(1)}, u32[]{:S(2)}, u32[]{:S(2)}) async-start(bf16[8,2,24576]{2,1,0:T(2,128)(2,1)} %reshape.49), calls=%async_computation.3 | async-start | bytes 1572864 | tf_op jit(solution)/shard_map/all_to_all | solution.py:84
Sparse Core Ops, SparseCore 0:
  10.2 45.4 all-gather.2
  57.8 39.7 all-gather.4
where the time goes:
time: 285 us
  waiting for transfers between devices  139 us (49%)
  blocking collectives  76 us (27%)
  starting transfers between devices  23.1 us (8%)
  between operations  14.3 us (5%)
  matrix products  14.2 us (5%)
  local copies, waits for them, and re-layouts  11.5 us (4%)
  other arithmetic  6.49 us (2%)
    all_to_all x1, blocking collectives, local(): lax.all_to_all(outgoing, 'slot', split_axis=0, concat_axis=1, tiled=True)  60.6 us
    all_to_all x1, waiting for transfers between devices, local(): lax.all_to_all(column_grad.astype(jnp.bfloat16), 'slot', split_axis=0, co...  49.9 us
    all_gather x1, waiting for transfers between devices, local(): piece = lax.all_gather(inputs, 'hid', axis=2, tiled=True)  45.1 us
    all_gather x1, waiting for transfers between devices, local(): column_piece = lax.all_gather(cotangent, 'hid', axis=2, tiled=True)  34.1 us
    all_to_all x1, starting transfers between devices, local(): lax.all_to_all(column_grad.astype(jnp.bfloat16), 'slot', split_axis=0, co...  15.4 us
    all_to_all x1, blocking collectives, local(): lax.all_to_all(slot_grad.astype(jnp.bfloat16), 'hid', split_axis=1, conca...  15.4 us
    all_to_all x1, waiting for transfers between devices, local(): lax.all_to_all(lax.all_to_all(outgoing, 'slot', split_axis=0, concat_axis...  8.54 us
    dot_general x8, matrix products, contract_cols(): lax.dot_general(left, right, (((1,), (1,)), ((), ())), preferred_element_...  7.7 us
  transfers between devices with their start and end apart: 4, of which 4 were waited for; matrix products, arithmetic and copies ran while one was open for 5% of the time, Pallas kernels for 0%

commit v1 on v0

v1 whole, which is shorter than its diff:
```python
import jax
import jax.numpy as jnp
from jax import lax
from jax.experimental import pallas as pl
from jax.experimental.pallas import tpu as pltpu
from jax.sharding import PartitionSpec as P

STEP = 100
Y, Z, X, CORES = 4, 16, 4, 2
SLOTS, HIDS = Y * Z, X * CORES
EXPERTS = 12
CAP = 512
WIDTH = 512
FEATURES = 4096
UNITS = 96
PIECE = (48, 128)
MESH = pl.DeviceIdType.MESH
F32, BF16 = jnp.float32, jnp.bfloat16


def remote(src, dst, send_sem, recv_sem, target):
    return pltpu.make_async_remote_copy(
        src_ref=src,
        dst_ref=dst,
        send_sem=send_sem,
        recv_sem=recv_sem,
        device_id=target,
        device_id_type=MESH,
    )


def wait_bytes(ref, sem):
    pltpu.make_async_copy(ref, ref, sem).wait()


def low_half(shape):
    return lax.broadcasted_iota(jnp.int32, shape, len(shape) - 2) < 4


def lanes(tile, q):
    return tile[..., 128 * q : 128 * (q + 1)]


def piece_tiles(whole, low, high):
    axis = len(whole.shape) - 2
    tiles = [lanes(whole, q) for q in range(4)]
    first = low_half(tiles[0].shape)
    for q in (0, 2):
        tiles.append(jnp.where(first, lanes(low, q), lanes(high, q + 1)))
    return jnp.concatenate(tiles, axis=axis)


def ring_gather(own, buf, half, sems, slot, hid, work):
    ring_send, ring_recv, mate_send, mate_recv = sems
    x, core = hid // CORES, hid % CORES
    right, left = lax.rem(x + 1, X), lax.rem(x + X - 1, X)
    across = lax.rem(x + 2, X)
    mate = hid + 1 - 2 * core
    ahead = ((slot, right * CORES + core), (slot, left * CORES + core))
    sources = (left, right)

    def part(ref, p):
        return ref.at[pl.ds(p * half, half)]

    started = []

    def start(src, block, p, send_sem, recv_sem, target):
        copy = remote(src, part(buf.at[block], p), send_sem, recv_sem, target)
        copy.start()
        started.append(copy)

    for step in range(2):
        for way in range(2):
            p = step if way == 0 else 1 - step
            start(part(own, p), hid, p, ring_send.at[way, step], ring_recv.at[way, step], ahead[way])
        start(part(own, step), hid, step, mate_send.at[step], mate_recv.at[step], (slot, mate))

    def arrival(step, way):
        chip = sources[way] if step < 2 else across
        p = (step if step < 2 else 0) if way == 0 else (1 - step if step < 2 else 1)
        return chip, p

    def expect(block, p, send_sem, recv_sem):
        ref = part(buf.at[block], p)
        remote(ref, ref, send_sem, recv_sem, (slot, mate)).wait_recv()

    work(hid, None)
    for step in range(3):
        for way in range(2):
            chip, p = arrival(step, way)
            block = chip * CORES + core
            expect(block, p, ring_send.at[way, step], ring_recv.at[way, step])
            ref = part(buf.at[block], p)
            if step == 0:
                start(ref, block, p, ring_send.at[way, 2], ring_recv.at[way, 2], ahead[way])
            at = 2 + 2 * step + way
            start(ref, block, p, mate_send.at[at], mate_recv.at[at], (slot, mate))
        if step == 0:
            for p in range(2):
                expect(mate, p, mate_send.at[p], mate_recv.at[p])
            work(mate, None)
        for way in range(2):
            chip, p = arrival(step, way)
            work(chip * CORES + core, p)
        for way in range(2):
            chip, p = arrival(step, way)
            at = 2 + 2 * step + way
            expect(chip * CORES + 1 - core, p, mate_send.at[at], mate_recv.at[at])
            work(chip * CORES + 1 - core, p)
    return started


def grads_kernel(
    counts_ref, place_ref, x_ref, cot_ref, gate_ref, up_ref, out_ref,
    xs, weights, cot, hidden, send, recv, sel, acc,
    load_sem, x_ring_send, x_ring_recv, x_mate_send, x_mate_recv,
    h_ring_send, h_ring_recv, h_mate_send, h_mate_recv, send_sem, recv_sem,
):
    slot, hid = lax.axis_index("slot"), lax.axis_index("hid")
    x, core = hid // CORES, hid % CORES
    loads = [
        pltpu.make_async_copy(x_ref.at[0], xs.at[hid], load_sem.at[0]),
        pltpu.make_async_copy(gate_ref.at[0], weights.at[pl.ds(0, UNITS)], load_sem.at[1]),
        pltpu.make_async_copy(up_ref.at[0], weights.at[pl.ds(UNITS, UNITS)], load_sem.at[2]),
        pltpu.make_async_copy(cot_ref.at[0], cot, load_sem.at[3]),
    ]
    for load in loads:
        load.start()
    barrier = pltpu.get_barrier_semaphore()
    right, left = lax.rem(x + 1, X), lax.rem(x + X - 1, X)
    for peer in (right * CORES + core, left * CORES + core, hid + 1 - 2 * core):
        pl.semaphore_signal(barrier, inc=1, device_id=(slot, peer), device_id_type=MESH)

    @pl.loop(1, SLOTS)
    def _(d):
        pl.semaphore_signal(barrier, inc=1, device_id=(lax.rem(slot + d, SLOTS), hid), device_id_type=MESH)

    pl.semaphore_wait(barrier, SLOTS - 1 + 3)

    for load in loads:
        load.wait()

    def project(block, p):
        columns = pl.ds(pl.multiple_of(block * WIDTH, WIDTH), WIDTH)
        rows = slice(None) if p is None else slice(p * CAP // 2, (p + 1) * CAP // 2)
        term = lax.dot_general(
            weights[:, columns], xs[block, rows, :], (((1,), (1,)), ((), ())), preferred_element_type=F32
        )
        if p is None:
            first = not begun
            begun.append(block)
            if first:
                acc[...] = term
                return
        acc[:, rows] += term

    begun = []
    started = ring_gather(
        x_ref.at[0], xs, CAP // 2, (x_ring_send, x_ring_recv, x_mate_send, x_mate_recv), slot, hid, project
    )

    expert_of = lax.broadcasted_iota(jnp.int32, (EXPERTS * 16, SLOTS), 0) // 16
    held = jnp.where(place_ref[...] == expert_of, 1.0, 0.0).astype(BF16)
    column = lax.broadcasted_iota(jnp.int32, (SLOTS, SLOTS * 16), 1) // 16
    spread = jnp.where(lax.broadcasted_iota(jnp.int32, column.shape, 0) == column, 1.0, 0.0).astype(BF16)
    wide = jnp.dot(held, spread, preferred_element_type=F32)
    same = (lax.broadcasted_iota(jnp.int32, wide.shape, 0) % 16) == (
        lax.broadcasted_iota(jnp.int32, wide.shape, 1) % 16
    )
    sel[...] = jnp.where(same, wide, 0.0).astype(BF16)

    gate, up = acc[:UNITS], acc[UNITS:]
    value = (gate / (1.0 + jnp.exp(-gate))) * up
    valid = lax.broadcasted_iota(jnp.int32, value.shape, 1) < counts_ref[slot]
    hidden[hid] = jnp.where(valid, value, 0.0).astype(BF16)

    def exchange(block, p):
        size = UNITS if p is None else UNITS // 2
        base = 0 if p is None else p * size
        terms = jnp.dot(hidden[block, base : base + size, :], cot[...], preferred_element_type=F32)
        for pair in range(size // 24):
            top = 24 * pair
            begin, middle, end = (terms[top + 8 * i : top + 8 * (i + 1)] for i in range(3))
            turned = pltpu.roll(middle, 4, 0)
            owner = block * (UNITS // 12) + (base + top) // 12
            send[owner] = piece_tiles(begin, middle, turned).astype(BF16)
            send[owner + 1] = piece_tiles(end, turned, middle).astype(BF16)
        first = block * (UNITS // 12) + base // 12

        @pl.loop(0, size // 12)
        def _(i):
            owner = first + i

            @pl.when(owner != slot)
            def _():
                remote(send.at[owner], recv.at[slot], send_sem, recv_sem, (owner, hid)).start()

    started += ring_gather(
        hidden.at[hid], hidden, UNITS // 2, (h_ring_send, h_ring_recv, h_mate_send, h_mate_recv), slot, hid, exchange
    )
    recv[slot] = send[slot]
    for copy in started:
        copy.wait_send()
    wait_bytes(recv.at[pl.ds(0, SLOTS - 1)], recv_sem)

    tiles = []
    for t in range(3):
        pieces = recv[:, 16 * t : 16 * (t + 1), :].reshape(SLOTS * 16, 128)
        total = jnp.dot(sel[...], pieces, preferred_element_type=F32).reshape(EXPERTS, 16, 128)
        tiles += [total[:, :8], total[:, 8:]]
    odd = slot % 2
    rest = [tiles[4], pltpu.roll(tiles[4], 4, 1), tiles[5], pltpu.roll(tiles[5], 4, 1)]
    for q in range(4):
        columns = slice(128 * q, 128 * (q + 1))

        @pl.when(odd == 0)
        def _():
            out_ref[:, 0:8, columns] = tiles[q]
            out_ref[:, 8:12, columns] = rest[q][:, :4]

        @pl.when(odd == 1)
        def _():
            out_ref[:, 4:12, columns] = tiles[q]
            out_ref[:, 0:4, columns] = rest[q][:, :4]

    wait_bytes(send.at[pl.ds(0, SLOTS - 1)], send_sem)


def summed_grads(counts, place_now, inputs, cotangent, w_gate, w_up):
    anywhere = pl.BlockSpec(memory_space=pltpu.HBM)
    dma = pltpu.SemaphoreType.DMA
    return pl.pallas_call(
        grads_kernel,
        out_shape=jax.ShapeDtypeStruct((EXPERTS, 12, WIDTH), F32),
        in_specs=[
            pl.BlockSpec(memory_space=pltpu.SMEM),
            pl.BlockSpec(memory_space=pltpu.VMEM),
            anywhere, anywhere, anywhere, anywhere,
        ],
        out_specs=pl.BlockSpec(memory_space=pltpu.VMEM),
        scratch_shapes=[
            pltpu.VMEM((HIDS, CAP, WIDTH), BF16),
            pltpu.VMEM((2 * UNITS, FEATURES), BF16),
            pltpu.VMEM((CAP, WIDTH), BF16),
            pltpu.VMEM((HIDS, UNITS, CAP), BF16),
            pltpu.VMEM((SLOTS,) + PIECE, BF16),
            pltpu.VMEM((SLOTS,) + PIECE, BF16),
            pltpu.VMEM((EXPERTS * 16, SLOTS * 16), BF16),
            pltpu.VMEM((2 * UNITS, CAP), F32),
            dma((4,)),
            dma((2, 3)), dma((2, 3)), dma((8,)), dma((8,)),
            dma((2, 3)), dma((2, 3)), dma((8,)), dma((8,)),
            dma, dma,
        ],
        compiler_params=pltpu.CompilerParams(
            collective_id=0, has_side_effects=True, vmem_limit_bytes=40 * 1024 * 1024
        ),
    )(counts, place_now, inputs, cotangent, w_gate, w_up)


def place_kernel(
    place_ref, master_ref, out_ref, buf, stage, land, ring_send, ring_recv, send_sem, recv_sem
):
    slot, hid = lax.axis_index("slot"), lax.axis_index("hid")
    y, z = slot // Z, slot % Z
    x = hid // CORES
    up, down = lax.rem(z + 1, Z), lax.rem(z + Z - 1, Z)
    diagonal = x == y

    barrier = pltpu.get_barrier_semaphore()
    for peer in (up, down):
        pl.semaphore_signal(barrier, inc=1, device_id=(y * Z + peer, hid), device_id_type=MESH)
    for source in range(HIDS):
        @pl.when(jnp.logical_or(jnp.logical_not(diagonal), source != hid))
        def _():
            pl.semaphore_signal(barrier, inc=1, device_id=(x * Z + z, source), device_id_type=MESH)

    @pl.when(diagonal)
    def _():
        pl.semaphore_wait(barrier, HIDS + 1)

    @pl.when(jnp.logical_not(diagonal))
    def _():
        pl.semaphore_wait(barrier, HIDS + 2)

    first, last = master_ref[:, 0:8, :], master_ref[:, 4:12, :]

    @pl.when(slot % 2 == 0)
    def _():
        buf[z] = piece_tiles(first, pltpu.roll(last, 4, 1), last).astype(BF16)

    @pl.when(slot % 2 == 1)
    def _():
        buf[z] = piece_tiles(last, first, pltpu.roll(first, 4, 1)).astype(BF16)

    group = EXPERTS // 2
    ahead = ((y * Z + up, hid), (y * Z + down, hid))
    started = []

    def hop(way, step, g):
        block = lax.rem(z + (Z - step if way == 0 else step), Z)
        ref = buf.at[block, pl.ds(g * group, group)]
        copy = remote(ref, ref, ring_send.at[way, step, g], ring_recv.at[way, step, g], ahead[way])
        copy.start()
        started.append(copy)

    def arrived(way, step, g):
        block = lax.rem(z + (Z - 1 - step if way == 0 else step + 1), Z)
        ref = buf.at[block, pl.ds(g * group, group)]
        remote(ref, ref, ring_send.at[way, step, g], ring_recv.at[way, step, g], ahead[way]).wait_recv()
        return block

    def deliver(block):
        half = block // (Z // 2)
        target = y * CORES + half
        for to in range(Y):
            expert = place_ref[to * Z + z]
            chosen = buf[block, 0]
            for e in range(1, EXPERTS):
                chosen = lax.select(expert == e, buf[block, e], chosen)
            stage[block, to] = chosen
            mine = jnp.logical_and(to == y, target == hid)

            @pl.when(mine)
            def _():
                land[hid, block % (Z // 2)] = chosen

            @pl.when(jnp.logical_not(mine))
            def _():
                remote(
                    stage.at[block, to], land.at[hid, block % (Z // 2)], send_sem, recv_sem, (to * Z + z, target)
                ).start()

    steps = Z // 2
    for g in range(2):
        for way in range(2):
            hop(way, 0, g)
    deliver(z)
    for step in range(steps):
        ready = []
        for g in range(2):
            for way in range(2):
                if step == steps - 1 and g != way:
                    continue
                ready.append(arrived(way, step, g))
                if step < steps - 2 or (step == steps - 2 and g == way):
                    hop(way, step + 1, g)
        deliver(ready[0])
        if step < steps - 1:
            deliver(ready[1])
    for copy in started:
        copy.wait_send()

    @pl.when(diagonal)
    def _():
        wait_bytes(stage.at[pl.ds(0, Z - 2)], send_sem)
        wait_bytes(land.at[pl.ds(0, HIDS - 1)], recv_sem)

    @pl.when(jnp.logical_not(diagonal))
    def _():
        wait_bytes(stage, send_sem)
        wait_bytes(land, recv_sem)

    half = low_half((8, 128))
    for source in range(HIDS):
        columns = []
        for pair in range(Z // 4):
            even, odd = land[source, 2 * pair].astype(F32), land[source, 2 * pair + 1].astype(F32)
            for q in range(4):
                b = slice(32 + 8 * (q // 2), 40 + 8 * (q // 2))
                if q % 2 == 0:
                    middle = jnp.where(half, even[b], pltpu.roll(odd[b], 4, 0))
                else:
                    middle = jnp.where(half, pltpu.roll(even[b], 4, 0), odd[b])
                columns.append((even[8 * q : 8 * q + 8], middle, odd[8 * q : 8 * q + 8]))
        for q in range(4):
            tall = [tile for pair in range(Z // 4) for tile in columns[4 * pair + q]]
            at = WIDTH * source + 128 * q
            out_ref[0, :, at : at + 128] = jnp.concatenate(tall, axis=0).astype(BF16)


def placed(place_next, new_master):
    dma = pltpu.SemaphoreType.DMA
    return pl.pallas_call(
        place_kernel,
        out_shape=jax.ShapeDtypeStruct((1, UNITS, FEATURES), BF16),
        in_specs=[pl.BlockSpec(memory_space=pltpu.SMEM), pl.BlockSpec(memory_space=pltpu.VMEM)],
        out_specs=pl.BlockSpec(memory_space=pltpu.VMEM),
        scratch_shapes=[
            pltpu.VMEM((Z, EXPERTS) + PIECE, BF16),
            pltpu.VMEM((Z, Y) + PIECE, BF16),
            pltpu.VMEM((HIDS, Z // 2) + PIECE, BF16),
            dma((2, Z // 2, 2)), dma((2, Z // 2, 2)), dma, dma,
        ],
        compiler_params=pltpu.CompilerParams(
            collective_id=1, has_side_effects=True, vmem_limit_bytes=40 * 1024 * 1024
        ),
    )(place_next, new_master)


def local(
    inputs, cotangent, w_gate, w_up, counts, place_now, place_next, master, moment_one, moment_two
):
    experts_now = place_now[:, 0]
    summed = summed_grads(counts, experts_now[None, :], inputs, cotangent, w_gate, w_up)
    match = experts_now[None, :] == jnp.arange(EXPERTS, dtype=jnp.int32)[:, None]
    rows = jnp.sum(jnp.where(match, counts[None, :], 0), axis=1)
    grad = summed / rows.astype(F32)[:, None, None]
    new_one = 0.9 * moment_one + 0.1 * grad
    new_two = 0.95 * moment_two + 0.05 * grad * grad
    fixed_one = 1.0 - 0.9**STEP
    fixed_two = 1.0 - 0.95**STEP
    new_master = master - 0.01 * (new_one / fixed_one) / (jnp.sqrt(new_two / fixed_two) + 1e-08)
    next_down = placed(place_next[:, 0], new_master)
    return (new_master, new_one, new_two, next_down)


def solution(mesh):
    sharded = P(None, "slot", "hid")
    return jax.shard_map(
        local,
        mesh=mesh,
        in_specs=(
            P("slot", None, "hid"),
            P("slot", None, "hid"),
            P("slot", "hid", None),
            P("slot", "hid", None),
            P(),
            P(),
            P(),
            sharded,
            sharded,
            sharded,
        ),
        out_specs=(sharded, sharded, sharded, P("slot", "hid", None)),
        check_vma=False,
    )
```

time: 285 us -> 135 us (0.47)
  waiting for transfers between devices: 139 us -> 0 us
  Pallas kernels: 0 us -> 126 us
  blocking collectives: 76 us -> 0 us
  starting transfers between devices: 23.1 us -> 0 us
  matrix products: 14.2 us -> 0 us
  between operations: 14.3 us -> 0.71 us
  other arithmetic: 6.49 us -> 1.34 us
  local copies, waits for them, and re-layouts: 11.5 us -> 6.55 us
    pallas_call x0 -> x2, Pallas kernels: none -> 126 us  [the longest x1 73.1 us: summed_grads(): pl.pallas_call(grads_kernel, out_shape=jax.ShapeDtypeStruct((EXPERTS, 12,...]
    all_gather x2 -> x0, waiting for transfers between devices: 79.2 us -> none  [the longest x1 45.1 us: local(): piece = lax.all_gather(inputs, 'hid', axis=2, tiled=True)]
    all_to_all x2 -> x0, blocking collectives: 76 us -> none  [the longest x1 60.6 us: local(): lax.all_to_all(outgoing, 'slot', split_axis=0, concat_axis=1, tiled=True)]
    all_to_all x2 -> x0, waiting for transfers between devices: 58.4 us -> none  [the longest x1 49.9 us: local(): lax.all_to_all(column_grad.astype(jnp.bfloat16), 'slot', split_axis=0, co...]
    all_to_all x2 -> x0, starting transfers between devices: 23 us -> none  [the longest x1 15.4 us: local(): lax.all_to_all(column_grad.astype(jnp.bfloat16), 'slot', split_axis=0, co...]
    dot_general x13 -> x0, matrix products: 14.2 us -> none  [the longest x8 7.7 us: contract_cols(): lax.dot_general(left, right, (((1,), (1,)), ((), ())), preferred_element_...]
    unnamed x1 -> x0, other arithmetic: 5.43 us -> none
    unnamed x31 -> x23, local copies, waits for them, and re-layouts: 6.8 us -> 6.55 us
  transfers between devices with their start and end apart: 4 -> 0, of which waited for: 4 -> 0; matrix products, arithmetic and copies ran while one was open for 5% -> 0% of each run, Pallas kernels for 0% -> 0%
where the time goes in v1:
time: 135 us
  Pallas kernels  126 us (93%)
  local copies, waits for them, and re-layouts  6.55 us (5%)
    pallas_call x1, Pallas kernels, summed_grads(): pl.pallas_call(grads_kernel, out_shape=jax.ShapeDtypeStruct((EXPERTS, 12,...  73.1 us
    pallas_call x1, Pallas kernels, placed(): pl.pallas_call(place_kernel, out_shape=jax.ShapeDtypeStruct((1, UNITS, FE...  53.3 us
    unnamed x23, local copies, waits for them, and re-layouts  6.55 us

profile of v1, /device:TPU:1, one launch (start us, length us, event | category | flops | bytes accessed | tf_op | source)
XLA Modules:
  0.0 135.0 jit_solution(8697292816995381090)
XLA Ops:
  0.6 0.0 copy-start.6
  0.6 0.0 copy-start.7
  0.7 0.6 copy-done.6
  1.3 0.0 copy-done.7
  1.3 0.1 select_reduce_fusion
  1.4 0.0 copy-start.1
  1.4 1.1 copy-done.1
  2.6 0.0 copy-start.2
  2.6 1.1 copy-done.2
  3.7 0.0 copy-start.3
  3.7 1.0 copy-done.3
  4.7 0.0 copy-start.4
  4.7 1.0 copy-done.4
  5.8 0.0 copy-start.8
  5.8 0.0 copy-start.9
  5.8 0.0 copy-start.10
  5.8 73.1 %shard_map.129 = f32[12,12,512]{2,1,0:T(8,128)S(1)} custom-call(s32[64]{0:T(128)S(1)} %copy-done.6, s32[1,64]{1,0:T(1,128)S(1)} %bitcast.5, bf16[1,512,512]{2,1,0:T(8,128)(2,1)S(1)} %copy-done.3, bf16[1,512,512]{2,1,0:T(8,128)(2,1)S(1)} %copy-done.4, bf16[1,96,4096]{2,1,0:T(8,128)(2,1)S(1)} %copy-done.1, bf16[1,96,4096]{2,1,0:T(8,128)(2,1)S(1)} %copy-done.2), custom_call_target="tpu_custom_call" | custom-call | tf_op jit(solution)/shard_map/pallas_call | solution.py:232
  78.9 0.0 copy-done.8
  78.9 0.0 copy-done.9
  78.9 0.0 copy-done.10
  78.9 1.2 divide_subtract_fusion
  80.2 0.0 copy-start
  80.2 0.0 copy-start.5
  80.2 0.7 copy-done.5
  80.8 53.3 %shard_map.130 = bf16[1,96,4096]{2,1,0:T(8,128)(2,1)S(1)} custom-call(s32[64]{0:T(128)S(1)} %bitcast.3, f32[12,12,512]{2,1,0:T(8,128)S(1)} %get-tuple-element.11.master_ref), custom_call_target="tpu_custom_call" | custom-call | tf_op jit(solution)/shard_map/pallas_call | solution.py:384
  134.1 0.0 copy-done
  134.1 0.9 copy.15
  (1 shorter events, 0.0 us)
Async XLA Ops:
  0.6 0.7 copy-start.6
  0.6 0.7 copy-start.7
  1.4 1.1 copy-start.1
  2.6 1.1 copy-start.2
  3.7 1.0 copy-start.3
  4.7 1.0 copy-start.4
  5.8 73.1 %copy-start.8 = (f32[12,12,512]{2,1,0:T(8,128)S(1)}, f32[12,12,512]{2,1,0:T(8,128)}, u32[]{:S(2)}) copy-start(f32[12,12,512]{2,1,0:T(8,128)} %param.17) | copy-start | bytes 884740
  5.8 73.1 %copy-start.9 = (f32[12,12,512]{2,1,0:T(8,128)S(1)}, f32[12,12,512]{2,1,0:T(8,128)}, u32[]{:S(2)}) copy-start(f32[12,12,512]{2,1,0:T(8,128)} %param.18) | copy-start | bytes 884740
  5.8 73.1 %copy-start.10 = (f32[12,12,512]{2,1,0:T(8,128)S(1)}, f32[12,12,512]{2,1,0:T(8,128)}, u32[]{:S(2)}) copy-start(f32[12,12,512]{2,1,0:T(8,128)} %param.19) | copy-start | bytes 884740
  80.2 54.0 %copy-start = (f32[12,12,512]{2,1,0:T(8,128)}, f32[12,12,512]{2,1,0:T(8,128)S(1)}, u32[]{:S(2)}) copy-start(f32[12,12,512]{2,1,0:T(8,128)S(1)} %get-tuple-element.11.master_ref) | copy-start | bytes 884740
  80.2 0.7 copy-start.5

commit v2 on v1

v2 whole, which is shorter than its diff:
```python
import jax
import jax.numpy as jnp
from jax import lax
from jax.experimental import pallas as pl
from jax.experimental.pallas import tpu as pltpu
from jax.sharding import PartitionSpec as P

STEP = 100
Y, Z, X, CORES = 4, 16, 4, 2
SLOTS, HIDS = Y * Z, X * CORES
EXPERTS = 12
CAP = 512
WIDTH = 512
FEATURES = 4096
UNITS = 96
PIECE = (48, 128)
NEAR = Z // 2 - 2
GROUPS = 3
LAG = 2
MESH = pl.DeviceIdType.MESH
F32, BF16 = jnp.float32, jnp.bfloat16


def adam(grad, master, one, two):
    new_one = 0.9 * one + 0.1 * grad
    new_two = 0.95 * two + 0.05 * grad * grad
    fixed_one, fixed_two = 1.0 - 0.9**STEP, 1.0 - 0.95**STEP
    return (master - 0.01 * (new_one / fixed_one) / (jnp.sqrt(new_two / fixed_two) + 1e-08), new_one, new_two)


def remote(src, dst, send_sem, recv_sem, target):
    return pltpu.make_async_remote_copy(
        src_ref=src,
        dst_ref=dst,
        send_sem=send_sem,
        recv_sem=recv_sem,
        device_id=target,
        device_id_type=MESH,
    )


def wait_bytes(ref, sem):
    pltpu.make_async_copy(ref, ref, sem).wait()


def low_half(shape):
    return lax.broadcasted_iota(jnp.int32, shape, len(shape) - 2) < 4


def lanes(tile, q):
    return tile[..., 128 * q : 128 * (q + 1)]


def piece_tiles(whole, low, high):
    axis = len(whole.shape) - 2
    tiles = [lanes(whole, q) for q in range(4)]
    first = low_half(tiles[0].shape)
    for q in (0, 2):
        tiles.append(jnp.where(first, lanes(low, q), lanes(high, q + 1)))
    return jnp.concatenate(tiles, axis=axis)


def ring_gather(own, buf, half, sems, slot, hid, work):
    ring_send, ring_recv, mate_send, mate_recv = sems
    x, core = hid // CORES, hid % CORES
    right, left = lax.rem(x + 1, X), lax.rem(x + X - 1, X)
    across = lax.rem(x + 2, X)
    mate = hid + 1 - 2 * core
    ahead = ((slot, right * CORES + core), (slot, left * CORES + core))
    sources = (left, right)

    def part(ref, p):
        return ref.at[pl.ds(p * half, half)]

    started = []

    def start(src, block, p, send_sem, recv_sem, target):
        copy = remote(src, part(buf.at[block], p), send_sem, recv_sem, target)
        copy.start()
        started.append(copy)

    for step in range(2):
        for way in range(2):
            p = step if way == 0 else 1 - step
            start(part(own, p), hid, p, ring_send.at[way, step], ring_recv.at[way, step], ahead[way])
        start(part(own, step), hid, step, mate_send.at[step], mate_recv.at[step], (slot, mate))

    def arrival(step, way):
        chip = sources[way] if step < 2 else across
        p = (step if step < 2 else 0) if way == 0 else (1 - step if step < 2 else 1)
        return chip, p

    def expect(block, p, send_sem, recv_sem):
        ref = part(buf.at[block], p)
        remote(ref, ref, send_sem, recv_sem, (slot, mate)).wait_recv()

    work(hid, None)
    for step in range(3):
        for way in range(2):
            chip, p = arrival(step, way)
            block = chip * CORES + core
            expect(block, p, ring_send.at[way, step], ring_recv.at[way, step])
            ref = part(buf.at[block], p)
            if step == 0:
                start(ref, block, p, ring_send.at[way, 2], ring_recv.at[way, 2], ahead[way])
            at = 2 + 2 * step + way
            start(ref, block, p, mate_send.at[at], mate_recv.at[at], (slot, mate))
        if step == 0:
            for p in range(2):
                expect(mate, p, mate_send.at[p], mate_recv.at[p])
            work(mate, None)
        for way in range(2):
            chip, p = arrival(step, way)
            work(chip * CORES + core, p)
        for way in range(2):
            chip, p = arrival(step, way)
            at = 2 + 2 * step + way
            expect(chip * CORES + 1 - core, p, mate_send.at[at], mate_recv.at[at])
            work(chip * CORES + 1 - core, p)
    return started


def step_kernel(
    counts_ref, held_ref, share_ref, next_ref, x_ref, cot_ref, gate_ref, up_ref, master_ref, one_ref, two_ref,
    grad_ref, out_ref,
    xs, weights, cot, hidden, send, recv, sel, rows, acc, grad, master, one, two, buf, stage, picked, far, farthest, column, land,
    load_sem, x_ring_send, x_ring_recv, x_mate_send, x_mate_recv,
    h_ring_send, h_ring_recv, h_mate_send, h_mate_recv, send_sem, recv_sem,
    ring_send, ring_recv, far_send, far_recv, y_send, y_recv, row_send, row_recv,
):
    slot, hid = lax.axis_index("slot"), lax.axis_index("hid")
    y, z = slot // Z, slot % Z
    loads = [
        pltpu.make_async_copy(x_ref.at[0], xs.at[hid], load_sem.at[0]),
        pltpu.make_async_copy(gate_ref.at[0], weights.at[pl.ds(0, UNITS)], load_sem.at[1]),
        pltpu.make_async_copy(up_ref.at[0], weights.at[pl.ds(UNITS, UNITS)], load_sem.at[2]),
        pltpu.make_async_copy(cot_ref.at[0], cot, load_sem.at[3]),
        pltpu.make_async_copy(master_ref, master, load_sem.at[4]),
        pltpu.make_async_copy(one_ref, one, load_sem.at[5]),
        pltpu.make_async_copy(two_ref, two, load_sem.at[6]),
    ]
    for load in loads:
        load.start()
    barrier = pltpu.get_barrier_semaphore()

    @pl.loop(1, HIDS)
    def _(d):
        pl.semaphore_signal(barrier, inc=1, device_id=(slot, lax.rem(hid + d, HIDS)), device_id_type=MESH)

    @pl.loop(1, SLOTS)
    def _(d):
        pl.semaphore_signal(barrier, inc=1, device_id=(lax.rem(slot + d, SLOTS), hid), device_id_type=MESH)

    pl.semaphore_wait(barrier, SLOTS - 1 + HIDS - 1)

    def prepare():
        for load in loads:
            load.wait()
        expert_of = lax.broadcasted_iota(jnp.int32, (EXPERTS * 16, SLOTS), 0) // 16
        match = held_ref[...] == expert_of
        total_rows = jnp.sum(jnp.where(match, share_ref[...].astype(F32), 0.0), axis=1, keepdims=True)
        rows[...] = jnp.broadcast_to(total_rows, rows.shape)
        held = jnp.where(match, 1.0, 0.0).astype(BF16)
        source_of = lax.broadcasted_iota(jnp.int32, (SLOTS, SLOTS * 16), 1) // 16
        spread = jnp.where(lax.broadcasted_iota(jnp.int32, source_of.shape, 0) == source_of, 1.0, 0.0).astype(BF16)
        wide = jnp.dot(held, spread, preferred_element_type=F32)
        same = (lax.broadcasted_iota(jnp.int32, wide.shape, 0) % 16) == (
            lax.broadcasted_iota(jnp.int32, wide.shape, 1) % 16
        )
        sel[...] = jnp.where(same, wide, 0.0).astype(BF16)

    def project(block, p):
        if p is None and not begun:
            prepare()
        columns = pl.ds(pl.multiple_of(block * WIDTH, WIDTH), WIDTH)
        rows = slice(None) if p is None else slice(p * CAP // 2, (p + 1) * CAP // 2)
        term = lax.dot_general(
            weights[:, columns], xs[block, rows, :], (((1,), (1,)), ((), ())), preferred_element_type=F32
        )
        if p is None:
            first = not begun
            begun.append(block)
            if first:
                acc[...] = term
                return
        acc[:, rows] += term

    begun = []
    started = ring_gather(
        x_ref.at[0], xs, CAP // 2, (x_ring_send, x_ring_recv, x_mate_send, x_mate_recv), slot, hid, project
    )

    gate, up = acc[:UNITS], acc[UNITS:]
    value = (gate / (1.0 + jnp.exp(-gate))) * up
    valid = lax.broadcasted_iota(jnp.int32, value.shape, 1) < counts_ref[slot]
    hidden[hid] = jnp.where(valid, value, 0.0).astype(BF16)

    def exchange(block, p):
        size = UNITS if p is None else UNITS // 2
        base = 0 if p is None else p * size
        terms = jnp.dot(hidden[block, base : base + size, :], cot[...], preferred_element_type=F32)
        for pair in range(size // 24):
            top = 24 * pair
            begin, middle, end = (terms[top + 8 * i : top + 8 * (i + 1)] for i in range(3))
            turned = pltpu.roll(middle, 4, 0)
            owner = block * (UNITS // 12) + (base + top) // 12
            send[owner] = piece_tiles(begin, middle, turned).astype(BF16)
            send[owner + 1] = piece_tiles(end, turned, middle).astype(BF16)
        first = block * (UNITS // 12) + base // 12
        count = size // 12

        @pl.loop(0, count)
        def _(i):
            owner = first + lax.rem(z + i, count)
            @pl.when(owner != slot)
            def _():
                remote(send.at[owner], recv.at[slot], send_sem, recv_sem, (owner, hid)).start()

    started += ring_gather(
        hidden.at[hid], hidden, UNITS // 2, (h_ring_send, h_ring_recv, h_mate_send, h_mate_recv), slot, hid, exchange
    )
    recv[slot] = send[slot]
    for copy in started:
        copy.wait_send()
    wait_bytes(recv.at[pl.ds(0, SLOTS - 1)], recv_sem)

    tiles = []
    for t in range(3):
        pieces = recv[:, 16 * t : 16 * (t + 1), :].reshape(SLOTS * 16, 128)
        total = jnp.dot(sel[...], pieces, preferred_element_type=F32) / rows[...]
        total = total.reshape(EXPERTS, 16, 128)
        tiles += [total[:, :8], total[:, 8:]]
    odd = slot % 2
    rest = [tiles[4], pltpu.roll(tiles[4], 4, 1), tiles[5], pltpu.roll(tiles[5], 4, 1)]
    for q in range(4):
        columns = slice(128 * q, 128 * (q + 1))

        @pl.when(odd == 0)
        def _():
            grad[:, 0:8, columns] = tiles[q]
            grad[:, 8:12, columns] = rest[q][:, :4]

        @pl.when(odd == 1)
        def _():
            grad[:, 4:12, columns] = tiles[q]
            grad[:, 0:4, columns] = rest[q][:, :4]

    mean = grad[...]
    grad_ref[...] = mean
    grad[...] = adam(mean, master[...], one[...], two[...])[0]

    up, down = lax.rem(z + 1, Z), lax.rem(z + Z - 1, Z)
    first, last = grad[:, 0:8, :], grad[:, 4:12, :]

    @pl.when(slot % 2 == 0)
    def _():
        buf[z] = piece_tiles(first, pltpu.roll(last, 4, 1), last).astype(BF16)

    @pl.when(slot % 2 == 1)
    def _():
        buf[z] = piece_tiles(last, first, pltpu.roll(first, 4, 1)).astype(BF16)

    group = EXPERTS // GROUPS
    ahead = ((y * Z + up, hid), (y * Z + down, hid))
    hops = []

    def reached(way, step):
        return lax.rem(z + (Z - 1 - step if way == 0 else step + 1), Z)

    def hop(way, step, g):
        block = z if step == 0 else reached(way, step - 1)
        ref = buf.at[block, pl.ds(g * group, group)]
        copy = remote(ref, ref, ring_send.at[way, step, g], ring_recv.at[way, step, g], ahead[way])
        copy.start()
        hops.append(copy)

    def pick(block, to, column_z):
        expert = next_ref[to * Z + column_z]
        chosen = buf[block, 0]
        for e in range(1, EXPERTS):
            chosen = lax.select(expert == e, buf[block, e], chosen)
        return chosen

    def far_copy(way, last):
        if last:
            src, dst = far.at[way, pl.ds(Y, Y // 2)], farthest.at[way]
        else:
            src, dst = picked.at[way], far.at[way]
        return remote(src, dst, far_send.at[way, last], far_recv.at[way, last], ahead[way])

    def to_column(block, source=None):
        for d in range(Y):
            to = lax.rem(y + d, Y)
            if source is None:
                chosen = pick(block, to, z)
                if d == 0:
                    column[y, block] = chosen
                    continue
                stage[d - 1, block] = chosen
                ref = stage.at[d - 1, block]
            else:
                ref = source(to)
                if d == 0:
                    column[y, block] = ref[...]
                    continue
            remote(ref, column.at[y, block], y_send, y_recv.at[d - 1, block], (to * Z + z, hid)).start()

    def to_row(block):
        half = block // (Z // 2)
        for d in range(Y):
            source = lax.rem(y + Y - d, Y)
            if d > 0:
                ref = column.at[source, block]
                remote(ref, ref, y_send, y_recv.at[d - 1, block], (slot, hid)).wait_recv()
            target = source * CORES + half

            @pl.when(target == hid)
            def _():
                land[hid, block % (Z // 2)] = column[source, block]

            @pl.when(target != hid)
            def _():
                remote(
                    column.at[source, block], land.at[hid, block % (Z // 2)], row_send, row_recv, (slot, target)
                ).start()

    for g in range(GROUPS):
        for way in range(2):
            hop(way, 0, g)
    to_column(z)
    behind = [[z]]
    for step in range(Z // 2):
        ready = [reached(way, step) for way in range(2)]
        if step < NEAR:
            for g in range(GROUPS):
                for way in range(2):
                    ref = buf.at[ready[way], pl.ds(g * group, group)]
                    remote(ref, ref, ring_send.at[way, step, g], ring_recv.at[way, step, g], ahead[way]).wait_recv()
                    if step < NEAR - 1:
                        hop(way, step + 1, g)
            if step == NEAR - 1:
                for way in range(2):
                    one_on, two_on = (lax.rem(z + Z + d * (1 - 2 * way), Z) for d in (1, 2))
                    for to in range(Y):
                        picked[way, to] = pick(ready[way], to, one_on)
                    for to in range(Y // 2):
                        picked[way, Y + to] = pick(ready[way], way * (Y // 2) + to, two_on)
                    hops.append(far_copy(way, 0))
                    hops[-1].start()
            for way in range(2):
                to_column(ready[way])
        elif step == NEAR:
            for way in range(2):
                far_copy(way, 0).wait_recv()
                hops.append(far_copy(way, 1))
                hops[-1].start()
            for way in range(2):
                to_column(ready[way], lambda to: far.at[way, to])
        else:
            for way in range(2):
                far_copy(way, 1).wait_recv()
            ready = ready[:1]
            to_column(ready[0], lambda to: farthest.at[to // (Y // 2), to % (Y // 2)])
        behind.append(ready)
        if step >= LAG - 1:
            for block in behind[step + 1 - LAG]:
                to_row(block)
    for blocks in behind[Z // 2 + 1 - LAG :]:
        for block in blocks:
            to_row(block)
    wait_bytes(land.at[pl.ds(0, HIDS - 1)], row_recv)

    half = low_half((8, 128))
    for source in range(HIDS):
        columns = []
        for pair in range(Z // 4):
            even, odd = land[source, 2 * pair].astype(F32), land[source, 2 * pair + 1].astype(F32)
            for q in range(4):
                b = slice(32 + 8 * (q // 2), 40 + 8 * (q // 2))
                if q % 2 == 0:
                    middle = jnp.where(half, even[b], pltpu.roll(odd[b], 4, 0))
                else:
                    middle = jnp.where(half, pltpu.roll(even[b], 4, 0), odd[b])
                columns.append((even[8 * q : 8 * q + 8], middle, odd[8 * q : 8 * q + 8]))
        for q in range(4):
            tall = [tile for pair in range(Z // 4) for tile in columns[4 * pair + q]]
            at = WIDTH * source + 128 * q
            out_ref[0, :, at : at + 128] = jnp.concatenate(tall, axis=0).astype(BF16)
    for copy in hops:
        copy.wait_send()
    wait_bytes(send.at[pl.ds(0, SLOTS - 1)], send_sem)
    wait_bytes(stage, y_send)
    wait_bytes(land.at[pl.ds(0, HIDS - 1)], row_send)


def local(
    inputs, cotangent, w_gate, w_up, counts, place_now, place_next, master, moment_one, moment_two
):
    dma = pltpu.SemaphoreType.DMA
    smem, vmem, hbm = (pl.BlockSpec(memory_space=m) for m in (pltpu.SMEM, pltpu.VMEM, pltpu.HBM))
    state = (EXPERTS, 12, WIDTH)
    update = pl.pallas_call(
        step_kernel,
        out_shape=[jax.ShapeDtypeStruct(state, F32)] + [jax.ShapeDtypeStruct((1, UNITS, FEATURES), BF16)],
        in_specs=[smem, vmem, vmem, smem] + [hbm] * 7,
        out_specs=[vmem] * 2,
        scratch_shapes=[
            pltpu.VMEM((HIDS, CAP, WIDTH), BF16),
            pltpu.VMEM((2 * UNITS, FEATURES), BF16),
            pltpu.VMEM((CAP, WIDTH), BF16),
            pltpu.VMEM((HIDS, UNITS, CAP), BF16),
            pltpu.VMEM((SLOTS,) + PIECE, BF16),
            pltpu.VMEM((SLOTS,) + PIECE, BF16),
            pltpu.VMEM((EXPERTS * 16, SLOTS * 16), BF16),
            pltpu.VMEM((EXPERTS * 16, 128), F32),
            pltpu.VMEM((2 * UNITS, CAP), F32),
            pltpu.VMEM(state, F32), pltpu.VMEM(state, F32), pltpu.VMEM(state, F32), pltpu.VMEM(state, F32),
            pltpu.VMEM((Z, EXPERTS) + PIECE, BF16),
            pltpu.VMEM((Y - 1, Z) + PIECE, BF16),
            pltpu.VMEM((2, Y + Y // 2) + PIECE, BF16),
            pltpu.VMEM((2, Y + Y // 2) + PIECE, BF16),
            pltpu.VMEM((2, Y // 2) + PIECE, BF16),
            pltpu.VMEM((Y, Z) + PIECE, BF16),
            pltpu.VMEM((HIDS, Z // 2) + PIECE, BF16),
            dma((7,)),
            dma((2, 3)), dma((2, 3)), dma((8,)), dma((8,)),
            dma((2, 3)), dma((2, 3)), dma((8,)), dma((8,)),
            dma, dma,
            dma((2, NEAR, GROUPS)), dma((2, NEAR, GROUPS)), dma((2, 2)), dma((2, 2)), dma, dma((Y - 1, Z)), dma, dma,
        ],
        compiler_params=pltpu.CompilerParams(
            collective_id=0, has_side_effects=True, vmem_limit_bytes=60 * 1024 * 1024
        ),
    )
    grad, next_down = update(
        counts, place_now[:, 0][None, :], counts[None, :], place_next[:, 0],
        inputs, cotangent, w_gate, w_up, master, moment_one, moment_two,
    )
    return adam(grad, master, moment_one, moment_two) + (next_down,)


def solution(mesh):
    sharded = P(None, "slot", "hid")
    return jax.shard_map(
        local,
        mesh=mesh,
        in_specs=(
            P("slot", None, "hid"),
            P("slot", None, "hid"),
            P("slot", "hid", None),
            P("slot", "hid", None),
            P(),
            P(),
            P(),
            sharded,
            sharded,
            sharded,
        ),
        out_specs=(sharded, sharded, sharded, P("slot", "hid", None)),
        check_vma=False,
    )
```

time: 135 us -> 126 us (0.933); the launches traced: 135 us -> 124 us
  Pallas kernels: 126 us -> 120 us
  local copies, waits for them, and re-layouts: 6.55 us -> 0.9 us
    pallas_call x2 -> x1, Pallas kernels: 126 us -> 120 us  [local(): update(counts, place_now[:, 0][None, :], counts[None, :], place_next[:, 0...]
    unnamed x23 -> x9, local copies, waits for them, and re-layouts: 6.55 us -> 0.9 us
where the time goes in v2:
time: 126 us; the launch traced here: 124 us
  Pallas kernels  120 us (95%)
  other arithmetic  2.24 us (2%)
    pallas_call x1, Pallas kernels, local(): update(counts, place_now[:, 0][None, :], counts[None, :], place_next[:, 0...  120 us

profile of v2, /device:TPU:1, one launch (start us, length us, event | category | flops | bytes accessed | tf_op | source)
XLA Modules:
  0.0 124.3 jit_solution(4193092445961533981)
XLA Ops:
  0.6 0.0 copy-start
  0.6 0.0 copy-start.1
  0.7 0.0 copy-start.2
  0.7 120.5 %shard_map.129 = (f32[12,12,512]{2,1,0:T(8,128)}, bf16[1,96,4096]{2,1,0:T(8,128)(2,1)}) custom-call(s32[64]{0:T(128)} %counts_ref.1, s32[1,64]{1,0:T(1,128)} %bitcast.4, s32[1,64]{1,0:T(1,128)} %bitcast.3, s32[64]{0:T(128)} %bitcast.5, bf16[1,512,512]{2,1,0:T(8,128)(2,1)} %x_ref.1, bf16[1,512,512]{2,1,0:T(8,128)(2,1)} %cot_ref.1, ...), custom_call_target="tpu_custom_call" | custom-call | tf_op jit(solution)/shard_map/pallas_call | solution.py:435
  121.1 0.0 copy-done
  121.2 0.0 copy-done.1
  121.2 0.0 copy-done.2
  121.2 0.0 copy-start.3
  121.2 2.2 %divide_subtract_fusion = (f32[12,12,512]{2,1,0:T(8,128)}, f32[12,12,512]{2,1,0:T(8,128)}, f32[12,12,512]{2,1,0:T(8,128)}) fusion(f32[12,12,512]{2,1,0:T(8,128)S(1)} %copy-done, f32[12,12,512]{2,1,0:T(8,128)} %get-tuple-element.6, f32[12,12,512]{2,1,0:T(8,128)S(1)} %copy-done.1, f32[12,12,512]{2,1,0:T(8,128)S(1)} %copy-done.2), kind=kLoop, calls=%fused_computation.2 | loop fusion | flops 884736 | bytes 2064384 | tf_op jit(solution)/shard_map/sub | solution.py:28
  123.4 0.0 copy-done.3
  123.4 0.9 copy.15
Async XLA Ops:
  0.6 120.5 %copy-start = (f32[12,12,512]{2,1,0:T(8,128)S(1)}, f32[12,12,512]{2,1,0:T(8,128)}, u32[]{:S(2)}) copy-start(f32[12,12,512]{2,1,0:T(8,128)} %master_ref.1) | copy-start | bytes 884740
  0.6 120.5 %copy-start.1 = (f32[12,12,512]{2,1,0:T(8,128)S(1)}, f32[12,12,512]{2,1,0:T(8,128)}, u32[]{:S(2)}) copy-start(f32[12,12,512]{2,1,0:T(8,128)} %one_ref.1) | copy-start | bytes 884740
  0.7 120.5 %copy-start.2 = (f32[12,12,512]{2,1,0:T(8,128)S(1)}, f32[12,12,512]{2,1,0:T(8,128)}, u32[]{:S(2)}) copy-start(f32[12,12,512]{2,1,0:T(8,128)} %two_ref.1) | copy-start | bytes 884740
  121.2 2.3 %copy-start.3 = (bf16[1,96,4096]{2,1,0:T(8,128)(2,1)S(1)}, bf16[1,96,4096]{2,1,0:T(8,128)(2,1)}, u32[]{:S(2)}) copy-start(bf16[1,96,4096]{2,1,0:T(8,128)(2,1)} %get-tuple-element.18) | copy-start | bytes 2359300

commit v3 on v2

--- a/solution.py
+++ b/solution.py
@@ -17,6 +17,7 @@
 NEAR = Z // 2 - 2
 GROUPS = 3
 LAG = 2
+MEET_AT = (1, 5, 9)
 MESH = pl.DeviceIdType.MESH
 F32, BF16 = jnp.float32, jnp.bfloat16
 
@@ -60,7 +61,19 @@
     return jnp.concatenate(tiles, axis=axis)
 
 
-def ring_gather(own, buf, half, sems, slot, hid, work):
+EVENLY = (
+    ("land", 0), ("beside", 0), ("near", 0), ("other", 0),
+    ("land", 1), ("near", 1), ("other", 1),
+    ("land", 2), ("near", 2), ("other", 2),
+)
+ACROSS_FIRST = (
+    ("land", 0), ("beside", 0), ("near", 0), ("land", 1),
+    ("land", 2), ("near", 2), ("other", 2),
+    ("other", 0), ("near", 1), ("other", 1),
+)
+
+
+def ring_gather(own, buf, half, sems, slot, hid, work, order):
     ring_send, ring_recv, mate_send, mate_recv = sems
     x, core = hid // CORES, hid % CORES
     right, left = lax.rem(x + 1, X), lax.rem(x + X - 1, X)
@@ -94,8 +107,7 @@
         ref = part(buf.at[block], p)
         remote(ref, ref, send_sem, recv_sem, (slot, mate)).wait_recv()
 
-    work(hid, None)
-    for step in range(3):
+    def land(step):
         for way in range(2):
             chip, p = arrival(step, way)
             block = chip * CORES + core
@@ -105,28 +117,38 @@
                 start(ref, block, p, ring_send.at[way, 2], ring_recv.at[way, 2], ahead[way])
             at = 2 + 2 * step + way
             start(ref, block, p, mate_send.at[at], mate_recv.at[at], (slot, mate))
-        if step == 0:
-            for p in range(2):
-                expect(mate, p, mate_send.at[p], mate_recv.at[p])
-            work(mate, None)
+
+    def near(step):
         for way in range(2):
             chip, p = arrival(step, way)
             work(chip * CORES + core, p)
+
+    def other(step):
         for way in range(2):
             chip, p = arrival(step, way)
             at = 2 + 2 * step + way
             expect(chip * CORES + 1 - core, p, mate_send.at[at], mate_recv.at[at])
             work(chip * CORES + 1 - core, p)
+
+    def beside(step):
+        for p in range(2):
+            expect(mate, p, mate_send.at[p], mate_recv.at[p])
+        work(mate, None)
+
+    work(hid, None)
+    moves = {"land": land, "near": near, "other": other, "beside": beside}
+    for move, step in order:
+        moves[move](step)
     return started
 
 
 def step_kernel(
     counts_ref, held_ref, share_ref, next_ref, x_ref, cot_ref, gate_ref, up_ref, master_ref, one_ref, two_ref,
     grad_ref, out_ref,
-    xs, weights, cot, hidden, send, recv, sel, rows, acc, grad, master, one, two, buf, stage, picked, far, farthest, column, land,
+    xs, weights, cot, hidden, send, recv, sel, rows, acc, grad, master, one, two, buf, stage, picked, far, farthest, column, gathered, land,
     load_sem, x_ring_send, x_ring_recv, x_mate_send, x_mate_recv,
     h_ring_send, h_ring_recv, h_mate_send, h_mate_recv, send_sem, recv_sem,
-    ring_send, ring_recv, far_send, far_recv, y_send, y_recv, row_send, row_recv,
+    ring_send, ring_recv, far_send, far_recv, y_send, y_recv, row_send, row_recv, met,
 ):
     slot, hid = lax.axis_index("slot"), lax.axis_index("hid")
     y, z = slot // Z, slot % Z
@@ -143,15 +165,26 @@
         load.start()
     barrier = pltpu.get_barrier_semaphore()
 
-    @pl.loop(1, HIDS)
-    def _(d):
-        pl.semaphore_signal(barrier, inc=1, device_id=(slot, lax.rem(hid + d, HIDS)), device_id_type=MESH)
-
-    @pl.loop(1, SLOTS)
-    def _(d):
-        pl.semaphore_signal(barrier, inc=1, device_id=(lax.rem(slot + d, SLOTS), hid), device_id_type=MESH)
-
-    pl.semaphore_wait(barrier, SLOTS - 1 + HIDS - 1)
+    x, core = hid // CORES, hid % CORES
+
+    def in_line(step):
+        return (y * Z + lax.rem(z + Z + step, Z), hid)
+
+    def in_row(step):
+        return (lax.rem(y + Y + step, Y) * Z + z, hid)
+
+    greeted = [(slot, lax.rem(x + step, X) * CORES + core) for step in (1, X - 1)] + [(slot, hid + 1 - 2 * core)]
+    rounds = [[in_line(step) for step in (1, 2, 3)], [in_line(step) for step in (4, 8, 12)], [in_row(step) for step in (1, 2, 3)]]
+    greeted += [in_line(-step) for step in (1, 2, 3, 4, 8, 12)] + [in_row(-step) for step in (1, 2, 3)]
+    for peer in greeted:
+        pl.semaphore_signal(barrier, inc=1, device_id=peer, device_id_type=MESH)
+    pl.semaphore_wait(barrier, len(greeted))
+
+    def meet(at):
+        if at > 0:
+            pl.semaphore_wait(met.at[at - 1], len(rounds[at - 1]))
+        for peer in rounds[at] if at < len(rounds) else ():
+            pl.semaphore_signal(met.at[at], inc=1, device_id=peer, device_id_type=MESH)
 
     def prepare():
         for load in loads:
@@ -170,6 +203,9 @@
         sel[...] = jnp.where(same, wide, 0.0).astype(BF16)
 
     def project(block, p):
+        calls.append(block)
+        if len(calls) in MEET_AT:
+            meet(MEET_AT.index(len(calls)))
         if p is None and not begun:
             prepare()
         columns = pl.ds(pl.multiple_of(block * WIDTH, WIDTH), WIDTH)
@@ -185,11 +221,12 @@
                 return
         acc[:, rows] += term
 
-    begun = []
+    begun, calls = [], []
     started = ring_gather(
-        x_ref.at[0], xs, CAP // 2, (x_ring_send, x_ring_recv, x_mate_send, x_mate_recv), slot, hid, project
+        x_ref.at[0], xs, CAP // 2, (x_ring_send, x_ring_recv, x_mate_send, x_mate_recv), slot, hid, project, EVENLY
     )
 
+    meet(len(rounds))
     gate, up = acc[:UNITS], acc[UNITS:]
     value = (gate / (1.0 + jnp.exp(-gate))) * up
     valid = lax.broadcasted_iota(jnp.int32, value.shape, 1) < counts_ref[slot]
@@ -217,7 +254,7 @@
                 remote(send.at[owner], recv.at[slot], send_sem, recv_sem, (owner, hid)).start()
 
     started += ring_gather(
-        hidden.at[hid], hidden, UNITS // 2, (h_ring_send, h_ring_recv, h_mate_send, h_mate_recv), slot, hid, exchange
+        hidden.at[hid], hidden, UNITS // 2, (h_ring_send, h_ring_recv, h_mate_send, h_mate_recv), slot, hid, exchange, ACROSS_FIRST
     )
     recv[slot] = send[slot]
     for copy in started:
@@ -288,47 +325,54 @@
             src, dst = picked.at[way], far.at[way]
         return remote(src, dst, far_send.at[way, last], far_recv.at[way, last], ahead[way])
 
-    def to_column(block, source=None):
+    def to_column(at, blocks, source):
         for d in range(Y):
             to = lax.rem(y + d, Y)
-            if source is None:
-                chosen = pick(block, to, z)
+            for way, block in enumerate(blocks):
+                chosen = source(way, block, to)
                 if d == 0:
-                    column[y, block] = chosen
-                    continue
-                stage[d - 1, block] = chosen
-                ref = stage.at[d - 1, block]
-            else:
-                ref = source(to)
-                if d == 0:
-                    column[y, block] = ref[...]
-                    continue
-            remote(ref, column.at[y, block], y_send, y_recv.at[d - 1, block], (to * Z + z, hid)).start()
-
-    def to_row(block):
-        half = block // (Z // 2)
-        for d in range(Y):
-            source = lax.rem(y + Y - d, Y)
+                    gathered[y, block] = chosen
+                else:
+                    stage[d - 1, at, way] = chosen
             if d > 0:
-                ref = column.at[source, block]
-                remote(ref, ref, y_send, y_recv.at[d - 1, block], (slot, hid)).wait_recv()
+                remote(
+                    stage.at[d - 1, at, pl.ds(0, len(blocks))],
+                    column.at[d - 1, at, pl.ds(0, len(blocks))],
+                    y_send, y_recv.at[d - 1, at], (to * Z + z, hid),
+                ).start()
+
+    def to_row(at, blocks):
+        for d in range(1, Y):
+            ref = column.at[d - 1, at, pl.ds(0, len(blocks))]
+            remote(ref, ref, y_send, y_recv.at[d - 1, at], (slot, hid)).wait_recv()
+            for way, block in enumerate(blocks):
+                gathered[lax.rem(y + Y - d, Y), block] = column[d - 1, at, way]
+        if at == Z // 2:
+            return
+        turn = (at + 1) // 2 * (1 if at % 2 == 0 else -1)
+        side = 1 - 2 * lax.rem(z, 2)
+        pair = lax.rem(z // 2 + side * turn + Z, Z // 2)
+        first, half = pair * 2, pair // (Z // 4)
+        for source in range(Y):
             target = source * CORES + half
+            place = pl.ds(lax.rem(first, Z // 2), 2)
 
             @pl.when(target == hid)
             def _():
-                land[hid, block % (Z // 2)] = column[source, block]
+                land[hid, place] = gathered[source, pl.ds(first, 2)]
 
             @pl.when(target != hid)
             def _():
                 remote(
-                    column.at[source, block], land.at[hid, block % (Z // 2)], row_send, row_recv, (slot, target)
+                    gathered.at[source, pl.ds(first, 2)], land.at[hid, place], row_send, row_recv, (slot, target)
                 ).start()
 
     for g in range(GROUPS):
         for way in range(2):
             hop(way, 0, g)
-    to_column(z)
-    behind = [[z]]
+    here = lambda way, block, to: pick(block, to, z)
+    to_column(Z // 2, [z], here)
+    behind = [(Z // 2, [z])]
     for step in range(Z // 2):
         ready = [reached(way, step) for way in range(2)]
         if step < NEAR:
@@ -347,27 +391,23 @@
                         picked[way, Y + to] = pick(ready[way], way * (Y // 2) + to, two_on)
                     hops.append(far_copy(way, 0))
                     hops[-1].start()
-            for way in range(2):
-                to_column(ready[way])
+            to_column(step, ready, here)
         elif step == NEAR:
             for way in range(2):
                 far_copy(way, 0).wait_recv()
                 hops.append(far_copy(way, 1))
                 hops[-1].start()
-            for way in range(2):
-                to_column(ready[way], lambda to: far.at[way, to])
+            to_column(step, ready, lambda way, block, to: far[way, to])
         else:
             for way in range(2):
                 far_copy(way, 1).wait_recv()
             ready = ready[:1]
-            to_column(ready[0], lambda to: farthest.at[to // (Y // 2), to % (Y // 2)])
-        behind.append(ready)
+            to_column(step, ready, lambda way, block, to: farthest[to // (Y // 2), to % (Y // 2)])
+        behind.append((step, ready))
         if step >= LAG - 1:
-            for block in behind[step + 1 - LAG]:
-                to_row(block)
-    for blocks in behind[Z // 2 + 1 - LAG :]:
-        for block in blocks:
-            to_row(block)
+            to_row(*behind[step + 1 - LAG])
+    for item in behind[Z // 2 + 1 - LAG :]:
+        to_row(*item)
     wait_bytes(land.at[pl.ds(0, HIDS - 1)], row_recv)
 
     half = low_half((8, 128))
@@ -389,7 +429,7 @@
     for copy in hops:
         copy.wait_send()
     wait_bytes(send.at[pl.ds(0, SLOTS - 1)], send_sem)
-    wait_bytes(stage, y_send)
+    wait_bytes(gathered.at[pl.ds(0, Y - 1)], y_send)
     wait_bytes(land.at[pl.ds(0, HIDS - 1)], row_send)
 
 
@@ -416,17 +456,19 @@
             pltpu.VMEM((2 * UNITS, CAP), F32),
             pltpu.VMEM(state, F32), pltpu.VMEM(state, F32), pltpu.VMEM(state, F32), pltpu.VMEM(state, F32),
             pltpu.VMEM((Z, EXPERTS) + PIECE, BF16),
-            pltpu.VMEM((Y - 1, Z) + PIECE, BF16),
+            pltpu.VMEM((Y - 1, Z // 2 + 1, 2) + PIECE, BF16),
             pltpu.VMEM((2, Y + Y // 2) + PIECE, BF16),
             pltpu.VMEM((2, Y + Y // 2) + PIECE, BF16),
             pltpu.VMEM((2, Y // 2) + PIECE, BF16),
+            pltpu.VMEM((Y - 1, Z // 2 + 1, 2) + PIECE, BF16),
             pltpu.VMEM((Y, Z) + PIECE, BF16),
             pltpu.VMEM((HIDS, Z // 2) + PIECE, BF16),
             dma((7,)),
             dma((2, 3)), dma((2, 3)), dma((8,)), dma((8,)),
             dma((2, 3)), dma((2, 3)), dma((8,)), dma((8,)),
             dma, dma,
-            dma((2, NEAR, GROUPS)), dma((2, NEAR, GROUPS)), dma((2, 2)), dma((2, 2)), dma, dma((Y - 1, Z)), dma, dma,
+            dma((2, NEAR, GROUPS)), dma((2, NEAR, GROUPS)), dma((2, 2)), dma((2, 2)), dma, dma((Y - 1, Z // 2 + 1)), dma, dma,
+            pltpu.SemaphoreType.REGULAR((3,)),
         ],
         compiler_params=pltpu.CompilerParams(
             collective_id=0, has_side_effects=True, vmem_limit_bytes=60 * 1024 * 1024

time: 126 us -> 124 us (0.984); the launches traced: 124 us -> 124 us
  no operation moved by 1% of the time
where the time goes in v3:
time: 124 us
  Pallas kernels  120 us (97%)
  other arithmetic  2.24 us (2%)
    pallas_call x1, Pallas kernels, local(): update(counts, place_now[:, 0][None, :], counts[None, :], place_next[:, 0...  120 us

profile of v3, /device:TPU:1, one launch (start us, length us, event | category | flops | bytes accessed | tf_op | source)
XLA Modules:
  0.0 124.3 jit_solution(16248733634560303894)
XLA Ops:
  0.6 0.0 copy-start
  0.6 0.0 copy-start.1
  0.7 0.0 copy-start.2
  0.7 120.5 %shard_map.129 = (f32[12,12,512]{2,1,0:T(8,128)}, bf16[1,96,4096]{2,1,0:T(8,128)(2,1)}) custom-call(s32[64]{0:T(128)} %counts_ref.1, s32[1,64]{1,0:T(1,128)} %bitcast.4, s32[1,64]{1,0:T(1,128)} %bitcast.3, s32[64]{0:T(128)} %bitcast.5, bf16[1,512,512]{2,1,0:T(8,128)(2,1)} %x_ref.1, bf16[1,512,512]{2,1,0:T(8,128)(2,1)} %cot_ref.1, ...), custom_call_target="tpu_custom_call" | custom-call | tf_op jit(solution)/shard_map/pallas_call | solution.py:477
  121.2 0.0 copy-done
  121.2 0.0 copy-done.1
  121.2 0.0 copy-done.2
  121.2 0.0 copy-start.3
  121.2 2.2 %divide_subtract_fusion = (f32[12,12,512]{2,1,0:T(8,128)}, f32[12,12,512]{2,1,0:T(8,128)}, f32[12,12,512]{2,1,0:T(8,128)}) fusion(f32[12,12,512]{2,1,0:T(8,128)S(1)} %copy-done, f32[12,12,512]{2,1,0:T(8,128)} %get-tuple-element.6, f32[12,12,512]{2,1,0:T(8,128)S(1)} %copy-done.1, f32[12,12,512]{2,1,0:T(8,128)S(1)} %copy-done.2), kind=kLoop, calls=%fused_computation.2 | loop fusion | flops 884736 | bytes 2064384 | tf_op jit(solution)/shard_map/sub | solution.py:29
  123.4 0.0 copy-done.3
  123.5 0.9 copy.15
Async XLA Ops:
  0.6 120.5 %copy-start = (f32[12,12,512]{2,1,0:T(8,128)S(1)}, f32[12,12,512]{2,1,0:T(8,128)}, u32[]{:S(2)}) copy-start(f32[12,12,512]{2,1,0:T(8,128)} %master_ref.1) | copy-start | bytes 884740
  0.6 120.5 %copy-start.1 = (f32[12,12,512]{2,1,0:T(8,128)S(1)}, f32[12,12,512]{2,1,0:T(8,128)}, u32[]{:S(2)}) copy-start(f32[12,12,512]{2,1,0:T(8,128)} %one_ref.1) | copy-start | bytes 884740
  0.7 120.5 %copy-start.2 = (f32[12,12,512]{2,1,0:T(8,128)S(1)}, f32[12,12,512]{2,1,0:T(8,128)}, u32[]{:S(2)}) copy-start(f32[12,12,512]{2,1,0:T(8,128)} %two_ref.1) | copy-start | bytes 884740
  121.2 2.3 %copy-start.3 = (bf16[1,96,4096]{2,1,0:T(8,128)(2,1)S(1)}, bf16[1,96,4096]{2,1,0:T(8,128)(2,1)}, u32[]{:S(2)}) copy-start(bf16[1,96,4096]{2,1,0:T(8,128)(2,1)} %get-tuple-element.18) | copy-start | bytes 2359300

commit v4 on v3

--- a/solution.py
+++ b/solution.py
@@ -15,7 +15,7 @@
 UNITS = 96
 PIECE = (48, 128)
 NEAR = Z // 2 - 2
-GROUPS = 3
+GROUPS = 4
 LAG = 2
 MEET_AT = (1, 5, 9)
 MESH = pl.DeviceIdType.MESH
@@ -148,7 +148,7 @@
     xs, weights, cot, hidden, send, recv, sel, rows, acc, grad, master, one, two, buf, stage, picked, far, farthest, column, gathered, land,
     load_sem, x_ring_send, x_ring_recv, x_mate_send, x_mate_recv,
     h_ring_send, h_ring_recv, h_mate_send, h_mate_recv, send_sem, recv_sem,
-    ring_send, ring_recv, far_send, far_recv, y_send, y_recv, row_send, row_recv, met,
+    ring_send, ring_recv, far_send, far_recv, y_send, y_recv, row_send, row_recv, direct_send, direct_recv, met,
 ):
     slot, hid = lax.axis_index("slot"), lax.axis_index("hid")
     y, z = slot // Z, slot % Z
@@ -261,42 +261,7 @@
         copy.wait_send()
     wait_bytes(recv.at[pl.ds(0, SLOTS - 1)], recv_sem)
 
-    tiles = []
-    for t in range(3):
-        pieces = recv[:, 16 * t : 16 * (t + 1), :].reshape(SLOTS * 16, 128)
-        total = jnp.dot(sel[...], pieces, preferred_element_type=F32) / rows[...]
-        total = total.reshape(EXPERTS, 16, 128)
-        tiles += [total[:, :8], total[:, 8:]]
-    odd = slot % 2
-    rest = [tiles[4], pltpu.roll(tiles[4], 4, 1), tiles[5], pltpu.roll(tiles[5], 4, 1)]
-    for q in range(4):
-        columns = slice(128 * q, 128 * (q + 1))
-
-        @pl.when(odd == 0)
-        def _():
-            grad[:, 0:8, columns] = tiles[q]
-            grad[:, 8:12, columns] = rest[q][:, :4]
-
-        @pl.when(odd == 1)
-        def _():
-            grad[:, 4:12, columns] = tiles[q]
-            grad[:, 0:4, columns] = rest[q][:, :4]
-
-    mean = grad[...]
-    grad_ref[...] = mean
-    grad[...] = adam(mean, master[...], one[...], two[...])[0]
-
     up, down = lax.rem(z + 1, Z), lax.rem(z + Z - 1, Z)
-    first, last = grad[:, 0:8, :], grad[:, 4:12, :]
-
-    @pl.when(slot % 2 == 0)
-    def _():
-        buf[z] = piece_tiles(first, pltpu.roll(last, 4, 1), last).astype(BF16)
-
-    @pl.when(slot % 2 == 1)
-    def _():
-        buf[z] = piece_tiles(last, first, pltpu.roll(first, 4, 1)).astype(BF16)
-
     group = EXPERTS // GROUPS
     ahead = ((y * Z + up, hid), (y * Z + down, hid))
     hops = []
@@ -352,22 +317,74 @@
         turn = (at + 1) // 2 * (1 if at % 2 == 0 else -1)
         side = 1 - 2 * lax.rem(z, 2)
         pair = lax.rem(z // 2 + side * turn + Z, Z // 2)
-        first, half = pair * 2, pair // (Z // 4)
+        first = pair * 2
+        send_row(first, 2)
+        if at == Z // 2 - 2:
+            send_row(lax.rem(z - 7 * side + Z, Z), 1)
+
+    def send_row(first, size):
+        here, there = pl.ds(first, size), pl.ds(lax.rem(first, Z // 2), size)
         for source in range(Y):
-            target = source * CORES + half
-            place = pl.ds(lax.rem(first, Z // 2), 2)
+            target = source * CORES + first // (Z // 2)
 
             @pl.when(target == hid)
             def _():
-                land[hid, place] = gathered[source, pl.ds(first, 2)]
+                land[hid, there] = gathered[source, here]
 
             @pl.when(target != hid)
             def _():
+                remote(gathered.at[source, here], land.at[hid, there], row_send, row_recv, (slot, target)).start()
+
+    def direct(block):
+        target = y * CORES + block // (Z // 2)
+        for to in range(Y):
+            ref = farthest.at[to // (Y // 2), to % (Y // 2)]
+            local_one = jnp.logical_and(to == y, target == hid)
+
+            @pl.when(local_one)
+            def _():
+                land[hid, lax.rem(block, Z // 2)] = ref[...]
+
+            @pl.when(jnp.logical_not(local_one))
+            def _():
                 remote(
-                    gathered.at[source, pl.ds(first, 2)], land.at[hid, place], row_send, row_recv, (slot, target)
+                    ref, land.at[hid, lax.rem(block, Z // 2)], direct_send, direct_recv, (to * Z + z, target)
                 ).start()
 
+    def update(part, lines):
+        tiles = []
+        for t in range(3):
+            pieces = recv[:, 16 * t : 16 * (t + 1), :].reshape(SLOTS * 16, 128)
+            total = jnp.dot(sel[lines, :], pieces, preferred_element_type=F32) / rows[lines, :]
+            total = total.reshape(group, 16, 128)
+            tiles += [total[:, :8], total[:, 8:]]
+        rest = [tiles[4], pltpu.roll(tiles[4], 4, 1), tiles[5], pltpu.roll(tiles[5], 4, 1)]
+        for q in range(4):
+            columns = slice(128 * q, 128 * (q + 1))
+
+            @pl.when(slot % 2 == 0)
+            def _():
+                grad_ref[part, 0:8, columns] = tiles[q]
+                grad_ref[part, 8:12, columns] = rest[q][:, :4]
+
+            @pl.when(slot % 2 == 1)
+            def _():
+                grad_ref[part, 4:12, columns] = tiles[q]
+                grad_ref[part, 0:4, columns] = rest[q][:, :4]
+
+        grad[part] = adam(grad_ref[part], master[part], one[part], two[part])[0]
+        first, last = grad[part, 0:8, :], grad[part, 4:12, :]
+
+        @pl.when(slot % 2 == 0)
+        def _():
+            buf[z, part] = piece_tiles(first, pltpu.roll(last, 4, 1), last).astype(BF16)
+
+        @pl.when(slot % 2 == 1)
+        def _():
+            buf[z, part] = piece_tiles(last, first, pltpu.roll(first, 4, 1)).astype(BF16)
+
     for g in range(GROUPS):
+        update(pl.ds(g * group, group), pl.ds(16 * g * group, 16 * group))
         for way in range(2):
             hop(way, 0, g)
     here = lambda way, block, to: pick(block, to, z)
@@ -401,14 +418,32 @@
         else:
             for way in range(2):
                 far_copy(way, 1).wait_recv()
-            ready = ready[:1]
-            to_column(step, ready, lambda way, block, to: farthest[to // (Y // 2), to % (Y // 2)])
-        behind.append((step, ready))
+            direct(ready[0])
+        if step < Z // 2 - 1:
+            behind.append((step, ready))
         if step >= LAG - 1:
             to_row(*behind[step + 1 - LAG])
     for item in behind[Z // 2 + 1 - LAG :]:
         to_row(*item)
-    wait_bytes(land.at[pl.ds(0, HIDS - 1)], row_recv)
+    far_here = lax.rem(z + Z // 2, Z) // (Z // 2) == core
+    near_only = jnp.logical_not(far_here)
+    diagonal = jnp.logical_and(far_here, x == y)
+
+    @pl.when(near_only)
+    def _():
+        wait_bytes(land.at[pl.ds(0, HIDS - 1)], row_recv)
+
+    @pl.when(far_here)
+    def _():
+        wait_bytes(land.at[pl.ds(0, HIDS - 1), pl.ds(0, Z // 2 - 1)], row_recv)
+
+    @pl.when(diagonal)
+    def _():
+        wait_bytes(recv.at[pl.ds(0, HIDS - 1)], direct_recv)
+
+    @pl.when(jnp.logical_and(far_here, x != y))
+    def _():
+        wait_bytes(recv.at[pl.ds(0, HIDS)], direct_recv)
 
     half = low_half((8, 128))
     for source in range(HIDS):
@@ -429,8 +464,24 @@
     for copy in hops:
         copy.wait_send()
     wait_bytes(send.at[pl.ds(0, SLOTS - 1)], send_sem)
-    wait_bytes(gathered.at[pl.ds(0, Y - 1)], y_send)
-    wait_bytes(land.at[pl.ds(0, HIDS - 1)], row_send)
+    wait_bytes(recv.at[pl.ds(0, (Y - 1) * (Z - 1))], y_send)
+    row_pieces = Y * (Z - 1) - Z // 2
+
+    @pl.when(near_only)
+    def _():
+        wait_bytes(recv.at[pl.ds(0, row_pieces)], row_send)
+
+    @pl.when(far_here)
+    def _():
+        wait_bytes(recv.at[pl.ds(0, row_pieces + 1)], row_send)
+
+    @pl.when(diagonal)
+    def _():
+        wait_bytes(recv.at[pl.ds(0, Y - 1)], direct_send)
+
+    @pl.when(jnp.logical_not(diagonal))
+    def _():
+        wait_bytes(recv.at[pl.ds(0, Y)], direct_send)
 
 
 def local(
@@ -467,7 +518,7 @@
             dma((2, 3)), dma((2, 3)), dma((8,)), dma((8,)),
             dma((2, 3)), dma((2, 3)), dma((8,)), dma((8,)),
             dma, dma,
-            dma((2, NEAR, GROUPS)), dma((2, NEAR, GROUPS)), dma((2, 2)), dma((2, 2)), dma, dma((Y - 1, Z // 2 + 1)), dma, dma,
+            dma((2, NEAR, GROUPS)), dma((2, NEAR, GROUPS)), dma((2, 2)), dma((2, 2)), dma, dma((Y - 1, Z // 2 + 1)), dma, dma, dma, dma,
             pltpu.SemaphoreType.REGULAR((3,)),
         ],
         compiler_params=pltpu.CompilerParams(

time: 124 us -> 122 us (0.984)
  Pallas kernels: 120 us -> 118 us
    pallas_call x1, Pallas kernels: 120 us -> 118 us  [local(): update(counts, place_now[:, 0][None, :], counts[None, :], place_next[:, 0...]
where the time goes in v4:
time: 122 us
  Pallas kernels  118 us (97%)
  other arithmetic  2.24 us (2%)
    pallas_call x1, Pallas kernels, local(): update(counts, place_now[:, 0][None, :], counts[None, :], place_next[:, 0...  118 us

profile of v4, /device:TPU:1, one launch (start us, length us, event | category | flops | bytes accessed | tf_op | source)
XLA Modules:
  0.0 122.3 jit_solution(10875403374043328127)
XLA Ops:
  0.6 0.0 copy-start
  0.6 0.0 copy-start.1
  0.7 0.0 copy-start.2
  0.7 118.5 %shard_map.129 = (f32[12,12,512]{2,1,0:T(8,128)}, bf16[1,96,4096]{2,1,0:T(8,128)(2,1)}) custom-call(s32[64]{0:T(128)} %counts_ref.1, s32[1,64]{1,0:T(1,128)} %bitcast.4, s32[1,64]{1,0:T(1,128)} %bitcast.3, s32[64]{0:T(128)} %bitcast.5, bf16[1,512,512]{2,1,0:T(8,128)(2,1)} %x_ref.1, bf16[1,512,512]{2,1,0:T(8,128)(2,1)} %cot_ref.1, ...), custom_call_target="tpu_custom_call" | custom-call | tf_op jit(solution)/shard_map/pallas_call | solution.py:528
  119.1 0.0 copy-done
  119.2 0.0 copy-done.1
  119.2 0.0 copy-done.2
  119.2 0.0 copy-start.3
  119.2 2.2 %divide_subtract_fusion = (f32[12,12,512]{2,1,0:T(8,128)}, f32[12,12,512]{2,1,0:T(8,128)}, f32[12,12,512]{2,1,0:T(8,128)}) fusion(f32[12,12,512]{2,1,0:T(8,128)S(1)} %copy-done, f32[12,12,512]{2,1,0:T(8,128)} %get-tuple-element.6, f32[12,12,512]{2,1,0:T(8,128)S(1)} %copy-done.1, f32[12,12,512]{2,1,0:T(8,128)S(1)} %copy-done.2), kind=kLoop, calls=%fused_computation.2 | loop fusion | flops 884736 | bytes 2064384 | tf_op jit(solution)/shard_map/sub | solution.py:29
  121.4 0.0 copy-done.3
  121.4 0.9 copy.15
Async XLA Ops:
  0.6 118.5 %copy-start = (f32[12,12,512]{2,1,0:T(8,128)S(1)}, f32[12,12,512]{2,1,0:T(8,128)}, u32[]{:S(2)}) copy-start(f32[12,12,512]{2,1,0:T(8,128)} %master_ref.1) | copy-start | bytes 884740
  0.6 118.5 %copy-start.1 = (f32[12,12,512]{2,1,0:T(8,128)S(1)}, f32[12,12,512]{2,1,0:T(8,128)}, u32[]{:S(2)}) copy-start(f32[12,12,512]{2,1,0:T(8,128)} %one_ref.1) | copy-start | bytes 884740
  0.7 118.5 %copy-start.2 = (f32[12,12,512]{2,1,0:T(8,128)S(1)}, f32[12,12,512]{2,1,0:T(8,128)}, u32[]{:S(2)}) copy-start(f32[12,12,512]{2,1,0:T(8,128)} %two_ref.1) | copy-start | bytes 884740
  119.2 2.3 %copy-start.3 = (bf16[1,96,4096]{2,1,0:T(8,128)(2,1)S(1)}, bf16[1,96,4096]{2,1,0:T(8,128)(2,1)}, u32[]{:S(2)}) copy-start(bf16[1,96,4096]{2,1,0:T(8,128)(2,1)} %get-tuple-element.18) | copy-start | bytes 2359300

commit v5 on v4

--- a/solution.py
+++ b/solution.py
@@ -16,8 +16,8 @@
 PIECE = (48, 128)
 NEAR = Z // 2 - 2
 GROUPS = 4
-LAG = 2
-MEET_AT = (1, 5, 9)
+LAG = 1
+MEET_AT = (1, 3, 7)
 MESH = pl.DeviceIdType.MESH
 F32, BF16 = jnp.float32, jnp.bfloat16
 
@@ -144,11 +144,11 @@
 
 def step_kernel(
     counts_ref, held_ref, share_ref, next_ref, x_ref, cot_ref, gate_ref, up_ref, master_ref, one_ref, two_ref,
-    grad_ref, out_ref,
-    xs, weights, cot, hidden, send, recv, sel, rows, acc, grad, master, one, two, buf, stage, picked, far, farthest, column, gathered, land,
+    mean_ref, out_ref,
+    xs, weights, cot, hidden, send, recv, sel, rows, acc, mean, placed, grad, master, one, two, buf, stage, picked, far, farthest, column, gathered, land,
     load_sem, x_ring_send, x_ring_recv, x_mate_send, x_mate_recv,
     h_ring_send, h_ring_recv, h_mate_send, h_mate_recv, send_sem, recv_sem,
-    ring_send, ring_recv, far_send, far_recv, y_send, y_recv, row_send, row_recv, direct_send, direct_recv, met,
+    ring_send, ring_recv, far_send, far_recv, y_send, y_recv, row_send, row_recv, direct_send, direct_recv, mean_sem, placed_sem, met,
 ):
     slot, hid = lax.axis_index("slot"), lax.axis_index("hid")
     y, z = slot // Z, slot % Z
@@ -364,15 +364,15 @@
 
             @pl.when(slot % 2 == 0)
             def _():
-                grad_ref[part, 0:8, columns] = tiles[q]
-                grad_ref[part, 8:12, columns] = rest[q][:, :4]
+                mean[part, 0:8, columns] = tiles[q]
+                mean[part, 8:12, columns] = rest[q][:, :4]
 
             @pl.when(slot % 2 == 1)
             def _():
-                grad_ref[part, 4:12, columns] = tiles[q]
-                grad_ref[part, 0:4, columns] = rest[q][:, :4]
-
-        grad[part] = adam(grad_ref[part], master[part], one[part], two[part])[0]
+                mean[part, 4:12, columns] = tiles[q]
+                mean[part, 0:4, columns] = rest[q][:, :4]
+
+        grad[part] = adam(mean[part], master[part], one[part], two[part])[0]
         first, last = grad[part, 0:8, :], grad[part, 4:12, :]
 
         @pl.when(slot % 2 == 0)
@@ -387,6 +387,8 @@
         update(pl.ds(g * group, group), pl.ds(16 * g * group, 16 * group))
         for way in range(2):
             hop(way, 0, g)
+    stores = [pltpu.make_async_copy(mean, mean_ref, mean_sem)]
+    stores[0].start()
     here = lambda way, block, to: pick(block, to, z)
     to_column(Z // 2, [z], here)
     behind = [(Z // 2, [z])]
@@ -460,9 +462,19 @@
         for q in range(4):
             tall = [tile for pair in range(Z // 4) for tile in columns[4 * pair + q]]
             at = WIDTH * source + 128 * q
-            out_ref[0, :, at : at + 128] = jnp.concatenate(tall, axis=0).astype(BF16)
+            placed[:, at : at + 128] = jnp.concatenate(tall, axis=0).astype(BF16)
+        stores.append(
+            pltpu.make_async_copy(
+                placed.at[:, pl.ds(WIDTH * source, WIDTH)],
+                out_ref.at[0, :, pl.ds(WIDTH * source, WIDTH)],
+                placed_sem.at[source],
+            )
+        )
+        stores[-1].start()
     for copy in hops:
         copy.wait_send()
+    for copy in stores:
+        copy.wait()
     wait_bytes(send.at[pl.ds(0, SLOTS - 1)], send_sem)
     wait_bytes(recv.at[pl.ds(0, (Y - 1) * (Z - 1))], y_send)
     row_pieces = Y * (Z - 1) - Z // 2
@@ -494,7 +506,7 @@
         step_kernel,
         out_shape=[jax.ShapeDtypeStruct(state, F32)] + [jax.ShapeDtypeStruct((1, UNITS, FEATURES), BF16)],
         in_specs=[smem, vmem, vmem, smem] + [hbm] * 7,
-        out_specs=[vmem] * 2,
+        out_specs=[hbm] * 2,
         scratch_shapes=[
             pltpu.VMEM((HIDS, CAP, WIDTH), BF16),
             pltpu.VMEM((2 * UNITS, FEATURES), BF16),
@@ -505,6 +517,7 @@
             pltpu.VMEM((EXPERTS * 16, SLOTS * 16), BF16),
             pltpu.VMEM((EXPERTS * 16, 128), F32),
             pltpu.VMEM((2 * UNITS, CAP), F32),
+            pltpu.VMEM(state, F32), pltpu.VMEM((UNITS, FEATURES), BF16),
             pltpu.VMEM(state, F32), pltpu.VMEM(state, F32), pltpu.VMEM(state, F32), pltpu.VMEM(state, F32),
             pltpu.VMEM((Z, EXPERTS) + PIECE, BF16),
             pltpu.VMEM((Y - 1, Z // 2 + 1, 2) + PIECE, BF16),
@@ -518,7 +531,7 @@
             dma((2, 3)), dma((2, 3)), dma((8,)), dma((8,)),
             dma((2, 3)), dma((2, 3)), dma((8,)), dma((8,)),
             dma, dma,
-            dma((2, NEAR, GROUPS)), dma((2, NEAR, GROUPS)), dma((2, 2)), dma((2, 2)), dma, dma((Y - 1, Z // 2 + 1)), dma, dma, dma, dma,
+            dma((2, NEAR, GROUPS)), dma((2, NEAR, GROUPS)), dma((2, 2)), dma((2, 2)), dma, dma((Y - 1, Z // 2 + 1)), dma, dma, dma, dma, dma, dma((HIDS,)),
             pltpu.SemaphoreType.REGULAR((3,)),
         ],
         compiler_params=pltpu.CompilerParams(

time: 122 us -> 122 us (level)
  no operation moved by 1% of the time
where the time goes in v5:
time: 122 us
  Pallas kernels  118 us (97%)
  other arithmetic  2.24 us (2%)
    pallas_call x1, Pallas kernels, local(): update(counts, place_now[:, 0][None, :], counts[None, :], place_next[:, 0...  118 us

profile of v5, /device:TPU:1, one launch (start us, length us, event | category | flops | bytes accessed | tf_op | source)
XLA Modules:
  0.0 121.6 jit_solution(9818821295048395246)
XLA Ops:
  0.6 0.0 copy-start
  0.6 0.0 copy-start.1
  0.7 0.0 copy-start.2
  0.7 117.7 %shard_map.129 = (f32[12,12,512]{2,1,0:T(8,128)}, bf16[1,96,4096]{2,1,0:T(8,128)(2,1)}) custom-call(s32[64]{0:T(128)} %counts_ref.1, s32[1,64]{1,0:T(1,128)} %bitcast.4, s32[1,64]{1,0:T(1,128)} %bitcast.3, s32[64]{0:T(128)} %bitcast.5, bf16[1,512,512]{2,1,0:T(8,128)(2,1)} %x_ref.1, bf16[1,512,512]{2,1,0:T(8,128)(2,1)} %cot_ref.1, ...), custom_call_target="tpu_custom_call" | custom-call | tf_op jit(solution)/shard_map/pallas_call | solution.py:541
  118.4 0.0 copy-done
  118.4 0.0 copy-done.1
  118.4 0.0 copy-done.2
  118.4 0.0 copy-start.3
  118.4 2.2 %divide_subtract_fusion = (f32[12,12,512]{2,1,0:T(8,128)}, f32[12,12,512]{2,1,0:T(8,128)}, f32[12,12,512]{2,1,0:T(8,128)}) fusion(f32[12,12,512]{2,1,0:T(8,128)S(1)} %copy-done, f32[12,12,512]{2,1,0:T(8,128)} %get-tuple-element.6, f32[12,12,512]{2,1,0:T(8,128)S(1)} %copy-done.1, f32[12,12,512]{2,1,0:T(8,128)S(1)} %copy-done.2), kind=kLoop, calls=%fused_computation.2 | loop fusion | flops 884736 | bytes 2064384 | tf_op jit(solution)/shard_map/sub | solution.py:29
  120.7 0.0 copy-done.3
  120.7 0.9 copy.15
Async XLA Ops:
  0.6 117.8 %copy-start = (f32[12,12,512]{2,1,0:T(8,128)S(1)}, f32[12,12,512]{2,1,0:T(8,128)}, u32[]{:S(2)}) copy-start(f32[12,12,512]{2,1,0:T(8,128)} %master_ref.1) | copy-start | bytes 884740
  0.6 117.8 %copy-start.1 = (f32[12,12,512]{2,1,0:T(8,128)S(1)}, f32[12,12,512]{2,1,0:T(8,128)}, u32[]{:S(2)}) copy-start(f32[12,12,512]{2,1,0:T(8,128)} %one_ref.1) | copy-start | bytes 884740
  0.7 117.8 %copy-start.2 = (f32[12,12,512]{2,1,0:T(8,128)S(1)}, f32[12,12,512]{2,1,0:T(8,128)}, u32[]{:S(2)}) copy-start(f32[12,12,512]{2,1,0:T(8,128)} %two_ref.1) | copy-start | bytes 884740
  118.4 2.3 %copy-start.3 = (bf16[1,96,4096]{2,1,0:T(8,128)(2,1)S(1)}, bf16[1,96,4096]{2,1,0:T(8,128)(2,1)}, u32[]{:S(2)}) copy-start(bf16[1,96,4096]{2,1,0:T(8,128)(2,1)} %get-tuple-element.18) | copy-start | bytes 2359300

commit v6 on v5

--- a/solution.py
+++ b/solution.py
@@ -65,11 +65,6 @@
     ("land", 0), ("beside", 0), ("near", 0), ("other", 0),
     ("land", 1), ("near", 1), ("other", 1),
     ("land", 2), ("near", 2), ("other", 2),
-)
-ACROSS_FIRST = (
-    ("land", 0), ("beside", 0), ("near", 0), ("land", 1),
-    ("land", 2), ("near", 2), ("other", 2),
-    ("other", 0), ("near", 1), ("other", 1),
 )
 
 
@@ -161,8 +156,6 @@
         pltpu.make_async_copy(one_ref, one, load_sem.at[5]),
         pltpu.make_async_copy(two_ref, two, load_sem.at[6]),
     ]
-    for load in loads:
-        load.start()
     barrier = pltpu.get_barrier_semaphore()
 
     x, core = hid // CORES, hid % CORES
@@ -178,6 +171,8 @@
     greeted += [in_line(-step) for step in (1, 2, 3, 4, 8, 12)] + [in_row(-step) for step in (1, 2, 3)]
     for peer in greeted:
         pl.semaphore_signal(barrier, inc=1, device_id=peer, device_id_type=MESH)
+    for load in loads:
+        load.start()
     pl.semaphore_wait(barrier, len(greeted))
 
     def meet(at):
@@ -254,7 +249,7 @@
                 remote(send.at[owner], recv.at[slot], send_sem, recv_sem, (owner, hid)).start()
 
     started += ring_gather(
-        hidden.at[hid], hidden, UNITS // 2, (h_ring_send, h_ring_recv, h_mate_send, h_mate_recv), slot, hid, exchange, ACROSS_FIRST
+        hidden.at[hid], hidden, UNITS // 2, (h_ring_send, h_ring_recv, h_mate_send, h_mate_recv), slot, hid, exchange, EVENLY
     )
     recv[slot] = send[slot]
     for copy in started:

time: 122 us -> 122 us (level)
  no operation moved by 1% of the time
where the time goes in v6:
time: 122 us
  Pallas kernels  118 us (97%)
  other arithmetic  2.24 us (2%)
    pallas_call x1, Pallas kernels, local(): update(counts, place_now[:, 0][None, :], counts[None, :], place_next[:, 0...  118 us

profile of v6, /device:TPU:1, one launch (start us, length us, event | category | flops | bytes accessed | tf_op | source)
XLA Modules:
  0.0 122.2 jit_solution(18289647049966586163)
XLA Ops:
  0.6 0.0 copy-start
  0.6 0.0 copy-start.1
  0.7 0.0 copy-start.2
  0.7 118.4 %shard_map.129 = (f32[12,12,512]{2,1,0:T(8,128)}, bf16[1,96,4096]{2,1,0:T(8,128)(2,1)}) custom-call(s32[64]{0:T(128)} %counts_ref.1, s32[1,64]{1,0:T(1,128)} %bitcast.4, s32[1,64]{1,0:T(1,128)} %bitcast.3, s32[64]{0:T(128)} %bitcast.5, bf16[1,512,512]{2,1,0:T(8,128)(2,1)} %x_ref.1, bf16[1,512,512]{2,1,0:T(8,128)(2,1)} %cot_ref.1, ...), custom_call_target="tpu_custom_call" | custom-call | tf_op jit(solution)/shard_map/pallas_call | solution.py:536
  119.1 0.0 copy-done
  119.1 0.0 copy-done.1
  119.1 0.0 copy-done.2
  119.1 0.0 copy-start.3
  119.1 2.2 %divide_subtract_fusion = (f32[12,12,512]{2,1,0:T(8,128)}, f32[12,12,512]{2,1,0:T(8,128)}, f32[12,12,512]{2,1,0:T(8,128)}) fusion(f32[12,12,512]{2,1,0:T(8,128)S(1)} %copy-done, f32[12,12,512]{2,1,0:T(8,128)} %get-tuple-element.6, f32[12,12,512]{2,1,0:T(8,128)S(1)} %copy-done.1, f32[12,12,512]{2,1,0:T(8,128)S(1)} %copy-done.2), kind=kLoop, calls=%fused_computation.2 | loop fusion | flops 884736 | bytes 2064384 | tf_op jit(solution)/shard_map/sub | solution.py:29
  121.4 0.0 copy-done.3
  121.4 0.9 copy.15
Async XLA Ops:
  0.6 118.4 %copy-start = (f32[12,12,512]{2,1,0:T(8,128)S(1)}, f32[12,12,512]{2,1,0:T(8,128)}, u32[]{:S(2)}) copy-start(f32[12,12,512]{2,1,0:T(8,128)} %master_ref.1) | copy-start | bytes 884740
  0.6 118.4 %copy-start.1 = (f32[12,12,512]{2,1,0:T(8,128)S(1)}, f32[12,12,512]{2,1,0:T(8,128)}, u32[]{:S(2)}) copy-start(f32[12,12,512]{2,1,0:T(8,128)} %one_ref.1) | copy-start | bytes 884740
  0.7 118.4 %copy-start.2 = (f32[12,12,512]{2,1,0:T(8,128)S(1)}, f32[12,12,512]{2,1,0:T(8,128)}, u32[]{:S(2)}) copy-start(f32[12,12,512]{2,1,0:T(8,128)} %two_ref.1) | copy-start | bytes 884740
  119.1 2.3 %copy-start.3 = (bf16[1,96,4096]{2,1,0:T(8,128)(2,1)S(1)}, bf16[1,96,4096]{2,1,0:T(8,128)(2,1)}, u32[]{:S(2)}) copy-start(bf16[1,96,4096]{2,1,0:T(8,128)(2,1)} %get-tuple-element.18) | copy-start | bytes 2359300
